TPU v7x, 256 devices: a whole 4x4x8 slice. The times are simulated.
256 devices in a mesh: ha: 64 (over z, y, core), ta: 4 (over x).
Axes of the slice: x: 4, y: 4, z: 8, core: 2. Of those that a mesh axis runs over, the one named last changes fastest.
Arguments:
- features: bfloat16 [32, 448, 224, 192], P('ta', 'ha'), may hold values from -6 to 6
- norm_gain: float32 [192], replicated, may hold values from 0.5 to 1.5
- head_weight: bfloat16 [3, 192, 27], replicated, may hold values from -0.078125 to 0.078125
- head_bias: float32 [3], replicated, may hold values from -0.5 to 0.5
- frame_order: int32 [32], replicated, may hold values from 0 to 31, each once
- patch_weight: bfloat16 [588, 1152], replicated, may hold values from -0.25 to 0.25
- patch_bias: float32 [1152], replicated, may hold values from -3 to 3
- pos_embed: bfloat16 [2048, 1152], P('ha'), may hold values from -3 to 3
- ln_gain: float32 [1152], replicated, may hold values from 0.5 to 1.5
- ln_bias: float32 [1152], replicated, may hold values from -3 to 3
- w_qkv: bfloat16 [1152, 1728], replicated, may hold values from -1.25 to 1.25
- b_qkv: float32 [1728], replicated, may hold values from -3 to 3
- w_out: bfloat16 [576, 1152], replicated, may hold values from -0.25 to 0.25
- b_out: float32 [1152], replicated, may hold values from -3 to 3
Outputs:
- encoded: bfloat16 [32, 2048, 1152], P('ta', 'ha')
Inputs may be any that keep to these rules, and one draw needn't show every extreme that they name: `frame_order`: each of the 32 frames appears once.
All inputs are finite; a program needn't handle non-finite values.
Results may differ from a plain program's by a relative error of at most 0.012.
Values may be sent and summed in bfloat16 or wider, within the bound.
A program may use at most 128 MiB of HBM per device.

v0:
```python
import math

import jax
import jax.numpy as jnp
from jax import lax
from jax.sharding import PartitionSpec as P

HEADS = 8
HD = 72


def with_halo(block, sides, width):
    for axis, dim in sides:
        count = lax.axis_size(axis)
        forward = [(i, i + 1) for i in range(count - 1)]
        backward = [(target, source) for source, target in forward]
        low = lax.ppermute(
            lax.slice_in_dim(block, block.shape[dim] - width, None, axis=dim), axis, forward
        )
        high = lax.ppermute(lax.slice_in_dim(block, 0, width, axis=dim), axis, backward)
        block = jnp.concatenate([low, block, high], axis=dim)
    return block


def passed_along(x, axis, by):
    count = lax.axis_size(axis)
    pairs = [(i, i + by) for i in range(count) if 0 <= i + by < count]
    return lax.ppermute(x, axis, pairs)


def activate(values, gain):
    widened = values.astype(jnp.float32)
    factor = lax.rsqrt(jnp.mean(widened * widened, axis=-1, keepdims=True) + 1e-06)
    return jax.nn.silu(widened * factor * gain).astype(jnp.bfloat16)


def assemble(taps):
    frame_count, rows_padded, cols_padded, taps_width = taps.shape
    grid = taps.reshape(frame_count, rows_padded, cols_padded, 3, 3, 3)
    inner_rows = rows_padded - 2
    inner_cols = cols_padded - 2
    row_parts = []
    for row_half in range(2):
        col_parts = []
        for col_half in range(2):
            summed = jnp.zeros((frame_count, inner_rows, inner_cols, 3), jnp.float32)
            for row_tap in range(3):
                top_row = 1 + (row_half + row_tap - 1) // 2
                for col_tap in range(3):
                    left_col = 1 + (col_half + col_tap - 1) // 2
                    summed = (
                        summed
                        + grid[
                            :,
                            top_row : top_row + inner_rows,
                            left_col : left_col + inner_cols,
                            row_tap,
                            col_tap,
                            :,
                        ]
                    )
            col_parts.append(summed)
        row_parts.append(jnp.stack(col_parts, axis=3))
    joined = jnp.stack(row_parts, axis=2)
    return joined.reshape(frame_count, 2 * inner_rows, 2 * inner_cols, 3)


def layer_norm(values, gain, shift_terms):
    widened = values.astype(jnp.float32)
    centre = jnp.mean(widened, axis=-1, keepdims=True)
    spread = jnp.mean((widened - centre) * (widened - centre), axis=-1, keepdims=True)
    return ((widened - centre) * lax.rsqrt(spread + 1e-06) * gain + shift_terms).astype(
        jnp.bfloat16
    )


def attend(block):
    items = block.shape[1]
    length = block.shape[2]
    split = block.reshape(items, length, 3, HD)
    queries = split[:, :, 0]
    keys_all = split[:, :, 1]
    values_all = split[:, :, 2]
    rows_step = math.gcd(length, 512)

    def one_block(start):
        query_rows = lax.dynamic_slice_in_dim(queries, start, rows_step, 1)
        scores = jnp.einsum(
            "gqd,gkd->gqk", query_rows, keys_all, preferred_element_type=jnp.float32
        ) * HD ** (-0.5)
        highest = jnp.max(scores, axis=-1, keepdims=True)
        expo = jnp.exp(scores - highest)
        weights = (expo / jnp.sum(expo, axis=-1, keepdims=True)).astype(jnp.bfloat16)
        return jnp.einsum(
            "gqk,gkd->gqd", weights, values_all, preferred_element_type=jnp.float32
        ).astype(jnp.bfloat16)

    starts = jnp.arange(length // rows_step, dtype=jnp.int32) * rows_step
    pieces = lax.map(one_block, starts)
    joined = jnp.transpose(pieces, (1, 0, 2, 3)).reshape(items, length, HD)
    return joined[None]


def shards(
    features,
    norm_gain,
    head_weight,
    head_bias,
    frame_order,
    patch_weight,
    patch_bias,
    pos_embed,
    ln_gain,
    ln_bias,
    w_qkv,
    b_qkv,
    w_out,
    b_out,
):
    frame_count, slab_rows, low_cols, channels = features.shape
    acted = activate(features, norm_gain)
    rimmed = with_halo(acted, (("ha", 1),), 1)
    rimmed = jnp.pad(rimmed, ((0, 0), (0, 0), (1, 1), (0, 0)))
    weight_cols = jnp.transpose(head_weight, (1, 0, 2)).reshape(channels, 81)
    prior = passed_along(rimmed[frame_count - 2 :], "ta", 1)
    frames_in = jnp.concatenate([prior, rimmed], axis=0)
    number = frames_in.shape[0]
    flat = jnp.dot(frames_in.reshape(-1, channels), weight_cols, preferred_element_type=jnp.float32)
    products = flat.reshape(number, slab_rows + 2, low_cols + 2, 3, 27)
    taps = (
        products[:frame_count, :, :, 0]
        + products[1 : frame_count + 1, :, :, 1]
        + products[2:, :, :, 2]
    )
    image = assemble(taps)
    image = image + head_bias
    side = 2 * slab_rows
    across = 2 * low_cols // side
    tiles = image.reshape(frame_count, side, across, side, 3).transpose(0, 2, 1, 3, 4)
    tiles = tiles.reshape(frame_count, across, side * side * 3).astype(jnp.bfloat16)
    every = lax.all_gather(tiles, "ta", axis=0, tiled=True)
    owned = lax.dynamic_slice_in_dim(
        frame_order, lax.axis_index("ta") * frame_count, frame_count, 0
    )
    mine = jnp.take(every, owned, axis=0)
    embedded = jnp.dot(
        mine.reshape(-1, mine.shape[2]), patch_weight, preferred_element_type=jnp.float32
    ).reshape(frame_count, across, -1)
    embedded = (embedded + patch_bias + pos_embed.astype(jnp.float32)).astype(jnp.bfloat16)
    width = embedded.shape[2]
    normed = layer_norm(embedded, ln_gain, ln_bias)
    projected = (
        jnp.dot(normed.reshape(-1, width), w_qkv, preferred_element_type=jnp.float32) + b_qkv
    )
    projected = projected.astype(jnp.bfloat16).reshape(frame_count, across, 3, HEADS, HD)
    slabs = lax.axis_size("ha")
    groups = frame_count * HEADS // slabs
    arranged = jnp.transpose(projected, (0, 3, 1, 2, 4)).reshape(slabs, groups, across, 3 * HD)
    context = attend(lax.all_to_all(arranged, "ha", split_axis=0, concat_axis=2, tiled=True))
    returned = lax.all_to_all(context, "ha", split_axis=2, concat_axis=0, tiled=True)
    merged = (
        returned.reshape(frame_count, HEADS, across, HD)
        .transpose(0, 2, 1, 3)
        .reshape(-1, HEADS * HD)
    )
    result = jnp.dot(merged, w_out, preferred_element_type=jnp.float32).reshape(
        frame_count, across, width
    )
    result = result + b_out + embedded.astype(jnp.float32)
    return result.astype(jnp.bfloat16)


def solution(mesh):
    in_specs = (
        P("ta", "ha", None, None),
        P(),
        P(),
        P(),
        P(),
        P(),
        P(),
        P("ha", None),
        P(),
        P(),
        P(),
        P(),
        P(),
        P(),
    )
    out_specs = P("ta", "ha", None)
    return jax.shard_map(shards, mesh=mesh, in_specs=in_specs, out_specs=out_specs, check_vma=False)
```

profile of v0, /device:TPU:1, one launch (start us, length us, event | category | flops | bytes accessed | tf_op | source)
XLA Modules:
  0.0 288.7 jit_solution(4329650071615759250)
XLA Ops:
  6.5 4.2 %fusion.13 = f32[8,7,224]{2,1,0:T(8,128)S(1)} fusion(bf16[8,7,224,192]{2,3,1,0:T(8,128)(2,1)} %param.16), kind=kLoop, calls=%fused_computation.21 | loop fusion | flops 7212800 | bytes 4867072 | tf_op jit(solution)/shard_map/reduce_sum | solution.py:33
  10.8 3.6 %fusion.20 = bf16[8,7,224,192]{2,3,1,0:T(8,128)(2,1)S(1)} fusion(bf16[8,7,224,192]{2,3,1,0:T(8,128)(2,1)S(1)} %copy-done.2, f32[192]{0:T(256)S(1)} %copy-done.13, f32[8,7,224]{2,1,0:T(8,128)S(1)} %add_rsqrt_fusion), kind=kLoop, calls=%fused_computation.28 | loop fusion | flops 19267584 | bytes 9684736 | tf_op jit(solution)/shard_map/convert_element_type | solution.py:34
  14.6 4.6 %collective-permute-start = (bf16[8,1,224,192]{2,3,1,0:T(8,128)(2,1)S(1)}, bf16[8,1,224,192]{2,3,1,0:T(8,128)(2,1)S(1)}, u32[]{:S(2)}, u32[]{:S(2)}) collective-permute-start(bf16[8,1,224,192]{2,3,1,0:T(8,128)(2,1)S(1)} %get-tuple-element.66), channel_id=1, source_target_pairs={{0,4},{4,8},{8,12},{12,16},{16,20},{20,24},{24,28},{28,32},{32,36}... | collective-permute-start | bytes 2064392 | tf_op jit(solution)/shard_map/ppermute | solution.py:17
  19.2 2.1 collective-permute-start.1
  21.3 6.8 %collective-permute-done = bf16[8,1,224,192]{2,3,1,0:T(8,128)(2,1)S(1)} collective-permute-done((bf16[8,1,224,192]{2,3,1,0:T(8,128)(2,1)S(1)}, bf16[8,1,224,192]{2,3,1,0:T(8,128)(2,1)S(1)}, u32[]{:S(2)}, u32[]{:S(2)}) %collective-permute-start) | collective-permute-done | bytes 688160 | tf_op jit(solution)/shard_map/ppermute | solution.py:17
  28.1 4.5 %collective-permute-done.1 = bf16[8,1,224,192]{2,3,1,0:T(8,128)(2,1)S(1)} collective-permute-done((bf16[8,1,224,192]{2,3,1,0:T(8,128)(2,1)S(1)}, bf16[8,1,224,192]{2,3,1,0:T(8,128)(2,1)S(1)}, u32[]{:S(2)}, u32[]{:S(2)}) %collective-permute-start.1) | collective-permute-done | bytes 688160 | tf_op jit(solution)/shard_map/ppermute | solution.py:20
  32.7 5.1 %fusion.28 = bf16[8,9,226,192]{2,3,1,0:T(8,128)(2,1)S(1)} fusion(bf16[8,1,224,192]{2,3,1,0:T(8,128)(2,1)S(1)} %collective-permute-done.1, bf16[8,7,224,192]{2,3,1,0:T(8,128)(2,1)S(1)} %fusion.20, bf16[8,1,224,192]{2,3,1,0:T(8,128)(2,1)S(1)} %collective-permute-done), kind=kLoop, calls=%fused_computation.38 | loop fusion | flops 37490688 | bytes 12441600 | tf_op jit(solution)/shard_map/concatenate | solution.py:21
  37.8 2.9 copy-done.3
  40.8 4.4 %collective-permute-start.2 = (bf16[2,9,226,192]{2,3,1,0:T(8,128)(2,1)S(1)}, bf16[2,9,226,192]{2,3,1,0:T(8,128)(2,1)}, u32[]{:S(2)}, u32[]{:S(2)}) collective-permute-start(bf16[2,9,226,192]{2,3,1,0:T(8,128)(2,1)S(1)} %slice.151), channel_id=1, source_target_pairs={{0,1},{1,2},{2,3},{4,5},{5,6},{6,7},{8,9},{9,10},{10,11},{12,13},{... | collective-permute-start | bytes 4686344 | tf_op jit(solution)/shard_map/ppermute | solution.py:28
  45.3 28.4 %collective-permute-done.2 = bf16[2,9,226,192]{2,3,1,0:T(8,128)(2,1)} collective-permute-done((bf16[2,9,226,192]{2,3,1,0:T(8,128)(2,1)S(1)}, bf16[2,9,226,192]{2,3,1,0:T(8,128)(2,1)}, u32[]{:S(2)}, u32[]{:S(2)}) %collective-permute-start.2) | collective-permute-done | bytes 1562144 | tf_op jit(solution)/shard_map/ppermute | solution.py:28
  73.7 4.4 %fusion.21 = f32[10,9,226,3,27]{2,4,3,1,0:T(8,128)S(1)} fusion(bf16[8,9,226,192]{2,3,1,0:T(8,128)(2,1)} %copy-done.3, bf16[2,9,226,192]{2,3,1,0:T(8,128)(2,1)} %collective-permute-done.2, bf16[3,27,192,1,1]{2,1,0,3,4:T(8,128)(2,1)S(1)} %reshape.518), kind=kOutput, calls=%fused_computation.31 | convolution fusion | flops 648276480 | bytes 14431824 | tf_op jit(solution)/shard_map/dot_general | solution.py:128
  78.9 1.2 copy.114
  81.6 8.2 %copy.140 = f32[8,7,2,224,2,3]{0,4,3,5,2,1:T(2,128)} copy(f32[8,7,2,224,2,3]{3,0,5,1,4,2:T(8,128)S(1)} %pad_maximum_fusion) | data formatting | bytes 1204224 | tf_op jit(solution)/shard_map/stack | solution.py:64
  89.8 12.8 %reshape.486 = f32[8,14,32,14,3]{0,3,2,4,1:T(8,128)} reshape(f32[8,7,2,224,2,3]{0,4,3,5,2,1:T(2,128)} %copy.140) | data formatting | bytes 1204224 | tf_op jit(solution)/shard_map/reshape | solution.py:65
  102.6 8.0 %fusion.29 = bf16[8,32,14,14,3]{0,3,1,4,2:T(8,128)(2,1)} fusion(f32[8,14,32,14,3]{0,3,2,4,1:T(8,128)} %reshape.486, f32[3]{0:T(128)S(1)} %copy-done.14), kind=kLoop, calls=%fused_computation.39 | loop fusion | flops 301056 | bytes 903180 | tf_op jit(solution)/shard_map/convert_element_type | solution.py:140
  110.6 7.0 %copy.141 = bf16[8,32,14,14,3]{1,0,4,3,2:T(8,128)(2,1)S(1)} copy(bf16[8,32,14,14,3]{0,3,1,4,2:T(8,128)(2,1)} %fusion.29) | data formatting | bytes 602112 | tf_op jit(solution)/shard_map/convert_element_type | solution.py:140
  117.6 1.6 copy.142
  119.4 37.3 %all-gather.2.cloned.1.call-done = bf16[32,32,588]{2,1,0:T(8,128)(2,1)} async-done(((bf16[8,32,588]{2,1,0:T(8,128)(2,1)}), bf16[32,32,588]{2,1,0:T(8,128)(2,1)}) %all-gather.2.cloned.1.call-update) | async-done | bytes 1204240 | tf_op jit(solution)/shard_map/all_gather | solution.py:141
  156.7 1.9 gather_fusion
  158.6 0.8 fusion.82
  161.2 1.4 fusion.35
  163.2 2.7 reshape.488
  165.8 2.5 copy.144
  168.3 2.2 reshape.489
  170.5 11.9 %all-to-all-start = ((bf16[64,1,32,216]{3,2,1,0:T(8,128)(2,1)}), bf16[64,1,32,216]{3,2,1,0:T(8,128)(2,1)S(1)}, u32[]{:S(2)}, u32[]{:S(2)}) async-start(bf16[64,1,32,216]{3,2,1,0:T(8,128)(2,1)} %bitcast.280), calls=%async_computation | async-start | bytes 2097152 | tf_op jit(solution)/shard_map/all_to_all | solution.py:159
  182.4 28.0 %all-to-all-done = bf16[64,1,32,216]{3,2,1,0:T(8,128)(2,1)S(1)} async-done(((bf16[64,1,32,216]{3,2,1,0:T(8,128)(2,1)}), bf16[64,1,32,216]{3,2,1,0:T(8,128)(2,1)S(1)}, u32[]{:S(2)}, u32[]{:S(2)}) %all-to-all-start) | async-done | bytes 884768 | tf_op jit(solution)/shard_map/all_to_all | solution.py:159
  210.4 1.1 reshape.490
  211.5 3.2 %fusion.81 = (bf16[1,2048,1,72]{3,2,1,0:T(2,128)(2,1)}, bf16[1,2048,1,72]{3,2,1,0:T(2,128)(2,1)S(1)}, bf16[1,2048,1,72]{3,2,1,0:T(2,128)(2,1)}) fusion(bf16[1,2048,3,72]{3,2,1,0:T(4,128)(2,1)S(1)} %reshape.490), kind=kLoop, calls=%fused_computation.133 | loop fusion | bytes 1769472 | tf_op jit(solution)/shard_map/slice | solution.py:83
  215.6 2.3 copy.148
  218.8 21.9 %while.10 = (s32[]{:T(128)}, bf16[4,1,512,72]{2,3,1,0:T(8,128)(2,1)S(1)}, s32[4]{0:T(128)S(1)}, bf16[1,2048,72]{1,2,0:T(8,128)(2,1)S(1)}, bf16[1,2048,72]{2,1,0:...) while((s32[]{:T(128)}, bf16[4,1,512,72]{2,3,1,0:T(8,128)(2,1)S(1)}, ...), condition=%wide.region_6.7_spmd, body=%wide.region_3.6_spmd.sunk | while | flops 311462912 | bytes 13789331 | solution.py:99
  221.4 1.0 multiply_reduce_fusion.3
  222.3 0.8 fusion.90
  223.1 1.1 fusion.91
  226.8 1.0 multiply_reduce_fusion.3
  227.8 0.8 fusion.90
  228.6 1.1 fusion.91
  232.3 1.0 multiply_reduce_fusion.3
  233.3 0.8 fusion.90
  234.1 1.1 fusion.91
  237.8 1.0 multiply_reduce_fusion.3
  238.7 0.8 fusion.90
  239.6 1.1 fusion.91
  241.8 11.5 %reduce.4 = bf16[2048,72]{1,0:T(8,128)(2,1)S(1)} reduce(bf16[2048,1,1,72]{3,2,1,0:T(2,128)(2,1)S(1)} %bitcast.281, bf16[]{:T(256)} %broadcast.107), dimensions={1,2}, to_apply=%bitcast.254.reduce_sub_computation | reduce | bytes 589826
  253.4 0.9 reshape.523
  254.3 20.1 %all_to_all.8 = bf16[64,2,1152]{2,1,0:T(2,128)(2,1)S(1)} all-to-all(bf16[64,2,1152]{2,1,0:T(2,128)(2,1)S(1)} %reshape.523), channel_id=1, replica_groups=mesh['ha'=64,'ta'=4] {'ha'}, dimensions={0} | all-to-all | bytes 589824 | tf_op jit(solution)/shard_map/all_to_all | solution.py:160
  274.4 2.7 reshape.524
  277.2 1.3 copy.160
  279.1 2.8 fusion.32
  (73 shorter events, 10.8 us)
Async XLA Ops:
  6.5 152.1 %copy-start = (bf16[588,1152]{1,0:T(8,128)(2,1)S(1)}, bf16[588,1152]{1,0:T(8,128)(2,1)}, u32[]{:S(2)}) copy-start(bf16[588,1152]{1,0:T(8,128)(2,1)} %param.21) | copy-start | bytes 4064260
  6.5 4.3 %copy-start.13 = (f32[192]{0:T(256)S(1)}, f32[192]{0:T(256)}, u32[]{:S(2)}) copy-start(f32[192]{0:T(256)} %param.17) | copy-start | bytes 2308
  6.5 150.1 %all-gather.2.cloned.1.call-start = ((), (), s32[]{:S(2)}) async-start(), calls=%async_computation.2 | async-start | bytes 1638400 | tf_op jit(solution)/shard_map/all_gather | solution.py:141
  6.5 4.3 %copy-start.2 = (bf16[8,7,224,192]{2,3,1,0:T(8,128)(2,1)S(1)}, bf16[8,7,224,192]{2,3,1,0:T(8,128)(2,1)}, u32[]{:S(2)}) copy-start(bf16[8,7,224,192]{2,3,1,0:T(8,128)(2,1)} %param.16) | copy-start | bytes 14450692
  14.6 13.5 %collective-permute-start = (bf16[8,1,224,192]{2,3,1,0:T(8,128)(2,1)S(1)}, bf16[8,1,224,192]{2,3,1,0:T(8,128)(2,1)S(1)}, u32[]{:S(2)}, u32[]{:S(2)}) collective-permute-start(bf16[8,1,224,192]{2,3,1,0:T(8,128)(2,1)S(1)} %get-tuple-element.66), channel_id=1, source_target_pairs={{0,4},{4,8},{8,12},{12,16},{16,20},{20,24},{24,28},{28,32},{32,36}... | collective-permute-start | bytes 2064392 | tf_op jit(solution)/shard_map/ppermute | solution.py:17
  19.2 26.1 %copy-start.9 = (bf16[3,192,27]{1,2,0:T(8,128)(2,1)S(1)}, bf16[3,192,27]{1,2,0:T(8,128)(2,1)}, u32[]{:S(2)}) copy-start(bf16[3,192,27]{1,2,0:T(8,128)(2,1)} %param.18) | copy-start | bytes 93316
  19.2 13.4 %collective-permute-start.1 = (bf16[8,1,224,192]{2,3,1,0:T(8,128)(2,1)S(1)}, bf16[8,1,224,192]{2,3,1,0:T(8,128)(2,1)S(1)}, u32[]{:S(2)}, u32[]{:S(2)}) collective-permute-start(bf16[8,1,224,192]{2,3,1,0:T(8,128)(2,1)S(1)} %get-tuple-element.67), channel_id=1, source_target_pairs={{4,0},{8,4},{12,8},{16,12},{20,16},{24,20},{28,24},{32,28},{36,32}... | collective-permute-start | bytes 2064392 | tf_op jit(solution)/shard_map/ppermute | solution.py:20
  37.8 2.9 copy-start.3
  40.8 32.9 %collective-permute-start.2 = (bf16[2,9,226,192]{2,3,1,0:T(8,128)(2,1)S(1)}, bf16[2,9,226,192]{2,3,1,0:T(8,128)(2,1)}, u32[]{:S(2)}, u32[]{:S(2)}) collective-permute-start(bf16[2,9,226,192]{2,3,1,0:T(8,128)(2,1)S(1)} %slice.151), channel_id=1, source_target_pairs={{0,1},{1,2},{2,3},{4,5},{5,6},{6,7},{8,9},{9,10},{10,11},{12,13},{... | collective-permute-start | bytes 4686344 | tf_op jit(solution)/shard_map/ppermute | solution.py:28
  89.8 12.8 %copy-start.14 = (f32[3]{0:T(128)S(1)}, f32[3]{0:T(128)}, u32[]{:S(2)}) copy-start(f32[3]{0:T(128)} %param.19) | copy-start | bytes 40
  110.6 8.6 %copy-start.8 = (bf16[32,1152]{1,0:T(8,128)(2,1)S(1)}, bf16[32,1152]{1,0:T(8,128)(2,1)}, u32[]{:S(2)}) copy-start(bf16[32,1152]{1,0:T(8,128)(2,1)} %param.23) | copy-start | bytes 221188
  110.6 8.7 %copy-start.15 = (s32[32]{0:T(128)S(1)}, s32[32]{0:T(128)}, u32[]{:S(2)}) copy-start(s32[32]{0:T(128)} %param.20) | copy-start | bytes 388
  110.6 48.0 %copy-start.17 = (f32[1152]{0:T(1024)S(1)}, f32[1152]{0:T(1024)}, u32[]{:S(2)}) copy-start(f32[1152]{0:T(1024)} %param.22) | copy-start | bytes 13828
  117.6 42.9 %copy-start.10 = (f32[1152]{0:T(1024)S(1)}, f32[1152]{0:T(1024)}, u32[]{:S(2)}) copy-start(f32[1152]{0:T(1024)} %param.25) | copy-start | bytes 13828
  117.6 42.9 %copy-start.11 = (f32[1152]{0:T(1024)S(1)}, f32[1152]{0:T(1024)}, u32[]{:S(2)}) copy-start(f32[1152]{0:T(1024)} %param.24) | copy-start | bytes 13828
  117.6 43.1 %copy-start.18 = (f32[1728]{0:T(1024)S(1)}, f32[1728]{0:T(1024)}, u32[]{:S(2)}) copy-start(f32[1728]{0:T(1024)} %param.27) | copy-start | bytes 20740
  158.6 2.6 copy-start.16
  159.5 1.0 copy-start.4
  170.5 39.9 %all-to-all-start = ((bf16[64,1,32,216]{3,2,1,0:T(8,128)(2,1)}), bf16[64,1,32,216]{3,2,1,0:T(8,128)(2,1)S(1)}, u32[]{:S(2)}, u32[]{:S(2)}) async-start(bf16[64,1,32,216]{3,2,1,0:T(8,128)(2,1)} %bitcast.280), calls=%async_computation | async-start | bytes 2097152 | tf_op jit(solution)/shard_map/all_to_all | solution.py:159
  214.7 3.5 %copy-start.6 = (bf16[1,2048,1,72]{3,2,1,0:T(2,128)(2,1)S(1)}, bf16[1,2048,1,72]{3,2,1,0:T(2,128)(2,1)}, u32[]{:S(2)}) copy-start(bf16[1,2048,1,72]{3,2,1,0:T(2,128)(2,1)} %get-tuple-element.70) | copy-start | bytes 884740
  214.7 4.1 %copy-start.7 = (bf16[4,1,512,72]{2,3,1,0:T(8,128)(2,1)S(1)}, bf16[4,1,512,72]{2,3,1,0:T(8,128)(2,1)}, u32[]{:S(2)}) copy-start(bf16[4,1,512,72]{2,3,1,0:T(8,128)(2,1)} %custom-call.2) | copy-start | bytes 884740
  241.3 37.8 %copy-start.5 = (f32[8,32,1152]{2,1,0:T(8,128)S(1)}, f32[8,32,1152]{2,1,0:T(8,128)}, u32[]{:S(2)}) copy-start(f32[8,32,1152]{2,1,0:T(8,128)} %copy-done.4) | copy-start | bytes 3538948
  241.3 37.8 %copy-start.12 = (f32[1152]{0:T(1024)S(1)}, f32[1152]{0:T(1024)}, u32[]{:S(2)}) copy-start(f32[1152]{0:T(1024)} %param.29) | copy-start | bytes 13828
  254.3 27.6 %copy-start.1 = (bf16[588,1152]{1,0:T(8,128)(2,1)S(1)}, bf16[588,1152]{1,0:T(8,128)(2,1)}, u32[]{:S(2)}) copy-start(bf16[588,1152]{1,0:T(8,128)(2,1)} %param.21) | copy-start | bytes 4064260
Sparse Core Ops, SparseCore 0:
  119.3 37.2 all-gather.1
where the time goes:
time: 290 us; the launch traced here: 289 us
  waiting for transfers between devices  105 us (36%)
  local copies, waits for them, and re-layouts  62.3 us (21%)
  other arithmetic  38.8 us (13%)
  starting transfers between devices  23 us (8%)
  blocking collectives  20.1 us (7%)
  matrix products  17.8 us (6%)
  between operations  13.9 us (5%)
  loops' own time  7.87 us (3%)
    all_gather x1, waiting for transfers between devices, shards(): every = lax.all_gather(tiles, 'ta', axis=0, tiled=True)  37.3 us
    ppermute x1, waiting for transfers between devices, passed_along(): return lax.ppermute(x, axis, pairs)  28.4 us
    all_to_all x1, waiting for transfers between devices, shards(): lax.all_to_all(arranged, 'ha', split_axis=0, concat_axis=2, tiled=True)  28 us
    all_to_all x1, blocking collectives, shards(): lax.all_to_all(context, 'ha', split_axis=2, concat_axis=0, tiled=True)  20.1 us
    reshape x1, local copies, waits for them, and re-layouts, assemble(): return joined.reshape(frame_count, 2 * inner_rows, 2 * inner_cols, 3)  12.8 us
    all_to_all x1, starting transfers between devices, shards(): lax.all_to_all(arranged, 'ha', split_axis=0, concat_axis=2, tiled=True)  11.9 us
    unnamed x1, other arithmetic  11.5 us
    unnamed x42, local copies, waits for them, and re-layouts  9.59 us
  transfers between devices with their start and end apart: 5, of which 5 were waited for; matrix products, arithmetic and copies ran while one was open for 0% of the time, Pallas kernels for 0%

commit v1 on v0

v1 whole, which is shorter than its diff:
```python
import functools

import jax
import jax.numpy as jnp
import numpy as np
from jax import lax
from jax.experimental import pallas as pl
from jax.experimental.pallas import tpu as pltpu
from jax.sharding import PartitionSpec as P

HEADS = 8
HD = 72
MESH = pl.DeviceIdType.MESH
F32 = jnp.float32
BF16 = jnp.bfloat16

P_ORDER = [0, 13] + list(range(1, 13))


def combine_matrix():
    m = np.zeros((256, 224), np.float32)
    for g in range(2):
        for j in range(3):
            shifted = 1 if (g == 0 and j == 0) or (g == 1 and j == 2) else 0
            base = shifted * 128 + g * 64
            for c in range(3):
                for at, p in enumerate(P_ORDER):
                    r, h = divmod(p, 2)
                    for i in range(3):
                        source = r + (h + i - 1) // 2
                        if 0 <= source < 7:
                            m[base + at * 3 + c, source * 32 + 9 * i + 3 * j + c] = 1
                m[base + 48 + c, 6 * 32 + 3 * j + c] = 1
                m[base + 56 + 3 + c, 18 + 3 * j + c] = 1
    return m.astype(jnp.bfloat16)


def column_matrix():
    m = np.zeros((224, 256), np.float32)
    for x in range(7):
        for token in range(32):
            m[x * 32 + token, 7 * token + x] = 1
    return m.astype(jnp.bfloat16)


def place_matrix():
    m = np.zeros((896, 640), np.float32)
    for x in range(7):
        for g in range(2):
            for at, p in enumerate(P_ORDER):
                for c in range(3):
                    m[x * 128 + g * 64 + at * 3 + c, 3 * (14 * p + 2 * x + g) + c] = 1
    return m.astype(jnp.bfloat16)


def greet(peers):
    barrier = pltpu.get_barrier_semaphore()
    for peer in peers:
        pl.semaphore_signal(barrier, inc=1, device_id=peer, device_id_type=MESH)
    pl.semaphore_wait(barrier, len(peers))


def remote(src, dst, send, recv, peer):
    return pltpu.make_async_remote_copy(
        src_ref=src, dst_ref=dst, send_sem=send, recv_sem=recv, device_id=peer, device_id_type=MESH
    )


def patches_kernel(
    x_hbm,
    taps_ref,
    gain_ref,
    bias_ref,
    order_ref,
    combine_ref,
    column_ref,
    place_ref,
    pos_ref,
    own_ref,
    pos_all_ref,
    x_ref,
    w_ref,
    acc,
    vs,
    edn,
    eup,
    vin,
    edn_c,
    eup_c,
    edn_in,
    eup_in,
    grid,
    gathered,
    pos_in,
    x_sem,
    send_sem,
    recv_sem,
):
    s = lax.axis_index("ha")
    t = lax.axis_index("ta")
    z = s // 8
    q = s % 8
    below = lax.rem(s + 1, 64)
    above = lax.rem(s + 63, 64)
    after = lax.rem(t + 1, 4)
    prior = lax.rem(t + 3, 4)

    loads = [pltpu.make_async_copy(x_hbm.at[f], x_ref.at[f], x_sem.at[f]) for f in range(8)]
    for f in [6, 7, 0, 1, 2, 3, 4, 5]:
        loads[f].start()

    ring = [{"ha": s, "ta": lax.rem(t + d, 4)} for d in range(1, 4)]
    column = [{"ha": lax.rem(z + d, 8) * 8 + q, "ta": t} for d in range(1, 8)]
    near = [
        {"ha": below, "ta": t},
        {"ha": above, "ta": t},
        {"ha": below, "ta": after},
        {"ha": above, "ta": after},
        {"ha": below, "ta": prior},
        {"ha": above, "ta": prior},
    ]
    greet(ring + column + near)

    pos_copies = []
    for d in range(7):
        copy = remote(pos_ref, pos_in.at[z], send_sem.at[8 + d], recv_sem.at[8 + d], column[d])
        copy.start()
        pos_copies.append(copy)

    w_ref[...] = jnp.zeros_like(w_ref)
    for tap in range(3):
        w_ref[tap, 0:27, :] = taps_ref[tap].astype(F32)
    acc[...] = jnp.zeros_like(acc)
    weight = w_ref[...].reshape(96, 192).astype(BF16)

    def convolve(f):
        for r in range(7):
            x = x_ref[f, r].astype(F32)
            factor = lax.rsqrt(jnp.sum(x * x, axis=0, keepdims=True) * (1.0 / 192.0) + 1e-06)
            u = x * factor * gain_ref[...]
            a = (u + u * jnp.tanh(u)).astype(BF16)
            res = jnp.dot(weight, a, preferred_element_type=F32)
            rows = pl.ds(r * 32, 32)
            acc[f, rows, 0:224] += res[64:96]
            acc[f + 1, rows, 0:224] += res[32:64]
            acc[f + 2, rows, 0:224] += res[0:32]

    def combine(f):
        total = acc[f]
        high = total.astype(BF16)
        low = (total - high.astype(F32)).astype(BF16)
        m = combine_ref[...]
        y = jnp.dot(m, high, preferred_element_type=F32) + jnp.dot(
            m, low, preferred_element_type=F32
        )
        for g in range(2):
            moved = pltpu.roll(y[128 + 64 * g : 192 + 64 * g], 1 if g == 0 else 255, 1)
            v = y[64 * g : 64 * g + 64] + moved
            vs[f, g] = v[0:48]
            edn[f, g] = v[48:56]
            eup[f, g] = v[56:64]

    def late(i, carry):
        f = i + 6
        pltpu.make_async_copy(x_hbm.at[f], x_ref.at[f], x_sem.at[f]).wait()
        convolve(f)
        return carry

    def early(f, carry):
        pltpu.make_async_copy(x_hbm.at[f], x_ref.at[f], x_sem.at[f]).wait()
        convolve(f)
        return carry

    lax.fori_loop(0, 2, late, 0)
    for f in (8, 9):
        combine(f)
    tail = pl.ds(8, 2)
    body = pl.ds(0, 8)
    halo = [
        remote(vs.at[tail], vin, send_sem.at[0], recv_sem.at[0], {"ha": s, "ta": after}),
        remote(edn.at[tail], edn_c, send_sem.at[1], recv_sem.at[1], near[2]),
        remote(eup.at[tail], eup_c, send_sem.at[2], recv_sem.at[2], near[3]),
        remote(edn.at[body], edn_in, send_sem.at[3], recv_sem.at[3], near[0]),
        remote(eup.at[body], eup_in, send_sem.at[4], recv_sem.at[4], near[1]),
    ]
    for copy in halo[:3]:
        copy.start()
    lax.fori_loop(0, 6, early, 0)

    def combine_one(f, carry):
        combine(f)
        return carry

    lax.fori_loop(0, 8, combine_one, 0)
    for copy in halo[3:]:
        copy.start()

    colour = lax.rem(lax.broadcasted_iota(jnp.int32, (48, 256), 0), 3)
    bias = jnp.where(colour == 0, bias_ref[0], jnp.where(colour == 1, bias_ref[1], bias_ref[2]))
    from_above = s > 0
    from_below = s < 63
    from_prior = t > 0
    for copy in halo:
        copy.wait()

    for f in range(2):
        for g in range(2):
            vs[f, g] += jnp.where(from_prior, vin[f, g], 0.0)
            vs[f, g, 0:8] += jnp.where(from_prior & from_above, edn_c[f, g], 0.0) + jnp.where(
                from_prior & from_below, eup_c[f, g], 0.0
            )

    def pixels(f, carry):
        parts = []
        for g in range(2):
            edge = jnp.where(from_above, edn_in[f, g], 0.0) + jnp.where(
                from_below, eup_in[f, g], 0.0
            )
            v = vs[f, g] + bias
            parts += [v[0:8] + edge, v[8:48], jnp.zeros((16, 256), F32)]
        v = jnp.concatenate(parts, axis=0).astype(BF16)
        cols = lax.dot_general(
            column_ref[...], v, (((1,), (1,)), ((), ())), preferred_element_type=F32
        ).astype(BF16)
        rows = pl.ds(pl.multiple_of(f * 32, 32), 32)
        for x in range(7):
            grid[rows, x * 128 : (x + 1) * 128] = cols[x * 32 : (x + 1) * 32]
        return carry

    lax.fori_loop(0, 8, pixels, 0)
    mine = pl.ds(t * 8, 8)
    gathered[mine] = (
        jnp.dot(grid[...], place_ref[...], preferred_element_type=F32)
        .astype(BF16)
        .reshape(8, 32, 640)
    )
    copies = []
    for d in range(3):
        copy = remote(
            gathered.at[mine], gathered.at[mine], send_sem.at[5 + d], recv_sem.at[5 + d], ring[d]
        )
        copy.start()
        copies.append(copy)
    for copy in pos_copies:
        copy.wait()
    pos_in[z] = pos_ref[...]
    pos_all_ref[...] = pos_in[...]
    for copy in copies:
        copy.wait()
    for j in range(8):
        own_ref[j] = gathered[order_ref[t * 8 + j]]


def patches(features, norm_gain, head_weight, head_bias, frame_order, pos_embed):
    x = jnp.transpose(features, (0, 1, 3, 2))
    taps = jnp.transpose(head_weight, (0, 2, 1))
    gain = jnp.broadcast_to(0.5 * norm_gain[:, None], (192, 224))
    vmem = pl.BlockSpec(memory_space=pltpu.VMEM)
    smem = pl.BlockSpec(memory_space=pltpu.SMEM)
    return pl.pallas_call(
        patches_kernel,
        out_shape=(
            jax.ShapeDtypeStruct((8, 32, 640), BF16),
            jax.ShapeDtypeStruct((8, 32, 1152), BF16),
        ),
        in_specs=[pl.BlockSpec(memory_space=pl.ANY), vmem, vmem, smem, smem, vmem, vmem, vmem, vmem],
        out_specs=(vmem, vmem),
        scratch_shapes=[
            pltpu.VMEM((8, 7, 192, 224), BF16),
            pltpu.VMEM((3, 32, 192), F32),
            pltpu.VMEM((10, 224, 256), F32),
            pltpu.VMEM((10, 2, 48, 256), F32),
            pltpu.VMEM((10, 2, 8, 256), F32),
            pltpu.VMEM((10, 2, 8, 256), F32),
            pltpu.VMEM((2, 2, 48, 256), F32),
            pltpu.VMEM((2, 2, 8, 256), F32),
            pltpu.VMEM((2, 2, 8, 256), F32),
            pltpu.VMEM((8, 2, 8, 256), F32),
            pltpu.VMEM((8, 2, 8, 256), F32),
            pltpu.VMEM((256, 896), BF16),
            pltpu.VMEM((32, 32, 640), BF16),
            pltpu.VMEM((8, 32, 1152), BF16),
            pltpu.SemaphoreType.DMA((8,)),
            pltpu.SemaphoreType.DMA((15,)),
            pltpu.SemaphoreType.DMA((15,)),
        ],
        compiler_params=pltpu.CompilerParams(
            collective_id=0, has_side_effects=True, vmem_limit_bytes=48 * 1024 * 1024
        ),
        name="patches",
    )(
        x,
        taps,
        gain,
        head_bias,
        frame_order,
        combine_matrix(),
        column_matrix(),
        place_matrix(),
        pos_embed,
    )


import math

def layer_norm(values, gain, shift_terms):
    widened = values.astype(jnp.float32)
    centre = jnp.mean(widened, axis=-1, keepdims=True)
    spread = jnp.mean((widened - centre) * (widened - centre), axis=-1, keepdims=True)
    return ((widened - centre) * lax.rsqrt(spread + 1e-06) * gain + shift_terms).astype(
        jnp.bfloat16
    )


def attend(block):
    items = block.shape[1]
    length = block.shape[2]
    split = block.reshape(items, length, 3, HD)
    queries = split[:, :, 0]
    keys_all = split[:, :, 1]
    values_all = split[:, :, 2]
    rows_step = math.gcd(length, 512)

    def one_block(start):
        query_rows = lax.dynamic_slice_in_dim(queries, start, rows_step, 1)
        scores = jnp.einsum(
            "gqd,gkd->gqk", query_rows, keys_all, preferred_element_type=jnp.float32
        ) * HD ** (-0.5)
        highest = jnp.max(scores, axis=-1, keepdims=True)
        expo = jnp.exp(scores - highest)
        weights = (expo / jnp.sum(expo, axis=-1, keepdims=True)).astype(jnp.bfloat16)
        return jnp.einsum(
            "gqk,gkd->gqd", weights, values_all, preferred_element_type=jnp.float32
        ).astype(jnp.bfloat16)

    starts = jnp.arange(length // rows_step, dtype=jnp.int32) * rows_step
    pieces = lax.map(one_block, starts)
    joined = jnp.transpose(pieces, (1, 0, 2, 3)).reshape(items, length, HD)
    return joined[None]


def shards(
    features,
    norm_gain,
    head_weight,
    head_bias,
    frame_order,
    patch_weight,
    patch_bias,
    pos_embed,
    ln_gain,
    ln_bias,
    w_qkv,
    b_qkv,
    w_out,
    b_out,
):
    own, pos_all = patches(features, norm_gain, head_weight, head_bias, frame_order, pos_embed)
    mine = own[:, :, :588]
    frame_count, across, _ = mine.shape
    embedded = jnp.dot(
        mine.reshape(-1, mine.shape[2]), patch_weight, preferred_element_type=jnp.float32
    ).reshape(frame_count, across, -1)
    embedded = (embedded + patch_bias + pos_embed.astype(jnp.float32)).astype(jnp.bfloat16)
    width = embedded.shape[2]
    normed = layer_norm(embedded, ln_gain, ln_bias)
    projected = (
        jnp.dot(normed.reshape(-1, width), w_qkv, preferred_element_type=jnp.float32) + b_qkv
    )
    projected = projected.astype(jnp.bfloat16).reshape(frame_count, across, 3, HEADS, HD)
    slabs = lax.axis_size("ha")
    groups = frame_count * HEADS // slabs
    arranged = jnp.transpose(projected, (0, 3, 1, 2, 4)).reshape(slabs, groups, across, 3 * HD)
    context = attend(lax.all_to_all(arranged, "ha", split_axis=0, concat_axis=2, tiled=True))
    returned = lax.all_to_all(context, "ha", split_axis=2, concat_axis=0, tiled=True)
    merged = (
        returned.reshape(frame_count, HEADS, across, HD)
        .transpose(0, 2, 1, 3)
        .reshape(-1, HEADS * HD)
    )
    result = jnp.dot(merged, w_out, preferred_element_type=jnp.float32).reshape(
        frame_count, across, width
    )
    result = result + b_out + embedded.astype(jnp.float32)
    return result.astype(jnp.bfloat16)


def solution(mesh):
    in_specs = (
        P("ta", "ha", None, None),
        P(),
        P(),
        P(),
        P(),
        P(),
        P(),
        P("ha", None),
        P(),
        P(),
        P(),
        P(),
        P(),
        P(),
    )
    out_specs = P("ta", "ha", None)
    return jax.shard_map(shards, mesh=mesh, in_specs=in_specs, out_specs=out_specs, check_vma=False)
```

time: 290 us -> 176 us (0.61)
  waiting for transfers between devices: 105 us -> 27.9 us
  Pallas kernels: 0 us -> 36.6 us
  local copies, waits for them, and re-layouts: 62.3 us -> 39.8 us
  other arithmetic: 38.8 us -> 17 us
  between operations: 13.9 us -> 0.32 us
  starting transfers between devices: 23 us -> 11.9 us
  matrix products: 17.8 us -> 13.3 us
    ppermute x3 -> x0, waiting for transfers between devices: 39.8 us -> none  [the longest x1 28.4 us: passed_along(): return lax.ppermute(x, axis, pairs)]
    all_gather x1 -> x0, waiting for transfers between devices: 37.3 us -> none  [shards(): every = lax.all_gather(tiles, 'ta', axis=0, tiled=True)]
    pallas_call x0 -> x1, Pallas kernels: none -> 36.6 us  [patches(): pl.pallas_call(patches_kernel, out_shape=(jax.ShapeDtypeStruct((8, 32, 64...]
    reshape x2 -> x0, local copies, waits for them, and re-layouts: 12.8 us -> none  [the longest x1 12.8 us: assemble(): return joined.reshape(frame_count, 2 * inner_rows, 2 * inner_cols, 3)]
    convert_element_type x2 -> x0, other arithmetic: 11.6 us -> none  [the longest x1 7.99 us: shards(): tiles.reshape(frame_count, across, side * side * 3).astype(jnp.bfloat16)]
    ppermute x3 -> x0, starting transfers between devices: 11.1 us -> none  [the longest x1 4.59 us: with_halo(): lax.ppermute(lax.slice_in_dim(block, block.shape[dim] - width, None, axis...]
    convert_element_type x2 -> x0, local copies, waits for them, and re-layouts: 8.56 us -> none  [shards(): tiles.reshape(frame_count, across, side * side * 3).astype(jnp.bfloat16)]
    another operation x1 -> x0, local copies, waits for them, and re-layouts: 8.18 us -> none  [assemble(): joined = jnp.stack(row_parts, axis=2)]
  transfers between devices with their start and end apart: 5 -> 1, of which waited for: 5 -> 1; matrix products, arithmetic and copies ran while one was open for 0% -> 0% of each run, Pallas kernels for 0% -> 0%
where the time goes in v1:
time: 176 us; the launch traced here: 175 us
  local copies, waits for them, and re-layouts  39.8 us (23%)
  Pallas kernels  36.6 us (21%)
  waiting for transfers between devices  27.9 us (16%)
  blocking collectives  20 us (11%)
  other arithmetic  17 us (10%)
  matrix products  13.3 us (8%)
  starting transfers between devices  11.9 us (7%)
  loops' own time  7.74 us (4%)
    pallas_call x1, Pallas kernels, patches(): pl.pallas_call(patches_kernel, out_shape=(jax.ShapeDtypeStruct((8, 32, 64...  36.6 us
    all_to_all x1, waiting for transfers between devices, shards(): lax.all_to_all(arranged, 'ha', split_axis=0, concat_axis=2, tiled=True)  27.9 us
    all_to_all x1, blocking collectives, shards(): lax.all_to_all(context, 'ha', split_axis=2, concat_axis=0, tiled=True)  20 us
    unnamed x40, local copies, waits for them, and re-layouts  12.9 us
    all_to_all x1, starting transfers between devices, shards(): lax.all_to_all(arranged, 'ha', split_axis=0, concat_axis=2, tiled=True)  11.9 us
    unnamed x1, other arithmetic  11.5 us
    another operation x1, loops' own time, attend(): pieces = lax.map(one_block, starts)  7.74 us
    slice x2, local copies, waits for them, and re-layouts, attend(): values_all = split[:, :, 2]  5.92 us
  transfers between devices with their start and end apart: 1, of which 1 were waited for; matrix products, arithmetic and copies ran while one was open for 0% of the time, Pallas kernels for 0%

profile of v1, /device:TPU:1, one launch (start us, length us, event | category | flops | bytes accessed | tf_op | source)
XLA Modules:
  0.0 174.5 jit_solution(2068239061693451304)
XLA Ops:
  0.0 0.8 broadcast_multiply_fusion.1
  0.8 0.9 convert_element_type.27
  1.8 1.2 copy-done.1
  3.0 0.9 copy-done.2
  3.9 0.9 copy-done.3
  4.8 0.9 copy-done.4
  5.7 0.8 copy-done.5
  6.5 0.7 copy-done.6
  7.2 0.7 copy-done.7
  7.8 36.6 %patches.1 = (bf16[8,32,640]{2,1,0:T(8,128)(2,1)S(1)}, bf16[8,32,1152]{2,1,0:T(8,128)(2,1)}) custom-call(bf16[8,7,192,224]{3,2,1,0:T(8,128)(2,1)} %bitcast.63, bf16[3,27,192]{2,1,0:T(8,128)(2,1)S(1)} %bitcast.61, f32[192,224]{1,0:T(8,128)S(1)} %broadcast_in_dim.8.gain_ref, f32[3]{0:T(128)S(1)} %copy-done.6, s32[32]{0:T(128)S(1)} %copy-done.7, ...), custom_call_target="tpu_custom_call" | custom-call | tf_op jit(solution)/shard_map/patches/pallas_call | solution.py:260
  44.5 0.7 fusion.22
  46.3 0.8 copy-done.16
  47.1 1.4 fusion.17
  48.4 0.6 copy.34
  49.0 2.7 %reshape.82 = bf16[8,32,3,8,72]{4,3,2,1,0:T(8,128)(2,1)} reshape(bf16[256,1728]{1,0:T(8,128)(2,1)S(1)} %copy.34) | data formatting | bytes 1769472 | tf_op jit(solution)/shard_map/reshape | solution.py:370
  51.7 2.5 %copy.35 = bf16[8,8,32,3,72]{4,3,2,1,0:T(4,128)(2,1)S(1)} copy(bf16[8,8,32,3,72]{4,1,3,2,0:T(8,128)(2,1)} %bitcast.62) | data formatting | bytes 1769472 | tf_op jit(solution)/shard_map/transpose | solution.py:373
  54.2 2.2 %reshape.83 = bf16[64,1,32,216]{3,2,0,1:T(8,128)(2,1)} reshape(bf16[8,8,32,3,72]{4,3,2,1,0:T(4,128)(2,1)S(1)} %copy.35) | data formatting | bytes 1769472 | tf_op jit(solution)/shard_map/reshape | solution.py:373
  56.4 11.9 %all-to-all-start = ((bf16[64,1,32,216]{3,2,1,0:T(8,128)(2,1)}), bf16[64,1,32,216]{3,2,1,0:T(8,128)(2,1)}, u32[]{:S(2)}, u32[]{:S(2)}) async-start(bf16[64,1,32,216]{3,2,1,0:T(8,128)(2,1)} %bitcast.64), calls=%async_computation | async-start | bytes 2097152 | tf_op jit(solution)/shard_map/all_to_all | solution.py:374
  68.4 27.9 %all-to-all-done = bf16[64,1,32,216]{3,2,1,0:T(8,128)(2,1)} async-done(((bf16[64,1,32,216]{3,2,1,0:T(8,128)(2,1)}), bf16[64,1,32,216]{3,2,1,0:T(8,128)(2,1)}, u32[]{:S(2)}, u32[]{:S(2)}) %all-to-all-start) | async-done | bytes 884768 | tf_op jit(solution)/shard_map/all_to_all | solution.py:374
  96.3 4.1 %reshape.84 = bf16[1,2048,3,72]{3,2,1,0:T(4,128)(2,1)S(1)} reshape(bf16[64,1,32,216]{3,2,1,0:T(8,128)(2,1)} %all-to-all-done) | data formatting | bytes 1769472 | tf_op jit(solution)/shard_map/reshape | solution.py:318
  100.4 3.6 %fusion.21 = (bf16[1,2048,1,72]{3,2,1,0:T(2,128)(2,1)}, bf16[1,2048,1,72]{3,2,1,0:T(2,128)(2,1)}, bf16[1,2048,1,72]{3,2,1,0:T(2,128)(2,1)}) fusion(bf16[1,2048,3,72]{3,2,1,0:T(4,128)(2,1)S(1)} %reshape.84), kind=kLoop, calls=%fused_computation.33 | loop fusion | bytes 1769472 | tf_op jit(solution)/shard_map/slice | solution.py:321
  104.0 2.3 %copy.38 = bf16[1,2048,1,72]{1,3,2,0:T(8,128)(2,1)S(1)} copy(bf16[1,2048,1,72]{3,2,1,0:T(2,128)(2,1)} %get-tuple-element.67) | data formatting | bytes 589824 | tf_op jit(solution)/shard_map/slice | solution.py:320
  106.6 2.3 %copy.39 = bf16[1,2048,1,72]{1,3,2,0:T(8,128)(2,1)S(1)} copy(bf16[1,2048,1,72]{3,2,1,0:T(2,128)(2,1)} %get-tuple-element.66) | data formatting | bytes 589824 | tf_op jit(solution)/shard_map/slice | solution.py:321
  108.9 1.0 copy.42
  109.9 0.6 copy.37
  110.5 22.9 %while.10 = (s32[]{:T(128)}, bf16[4,1,512,72]{2,3,1,0:T(8,128)(2,1)S(1)}, s32[4]{0:T(128)S(1)}, bf16[1,2048,72]{1,2,0:T(8,128)(2,1)S(1)}, bf16[1,2048,72]{2,1,0:...) while((s32[]{:T(128)}, bf16[4,1,512,72]{2,3,1,0:T(8,128)(2,1)S(1)}, ...), condition=%wide.region_5.6_spmd, body=%wide.region_2.5_spmd.sunk | while | flops 311462912 | bytes 14969007 | solution.py:337
  110.5 0.7 dynamic_slice.16
  113.1 1.0 multiply_reduce_fusion.3
  114.1 0.8 fusion.30
  115.1 1.1 fusion.31
  116.3 0.7 dynamic_slice.16
  118.8 1.0 multiply_reduce_fusion.3
  119.8 0.8 fusion.30
  120.8 1.1 fusion.31
  122.0 0.7 dynamic_slice.16
  124.5 1.0 multiply_reduce_fusion.3
  125.5 0.8 fusion.30
  126.5 1.1 fusion.31
  127.7 0.7 dynamic_slice.16
  130.3 1.0 multiply_reduce_fusion.3
  131.2 0.8 fusion.30
  132.3 1.1 fusion.31
  134.5 11.5 %reduce.4 = bf16[2048,72]{1,0:T(8,128)(2,1)S(1)} reduce(bf16[2048,1,1,72]{3,2,1,0:T(2,128)(2,1)S(1)} %bitcast.65, bf16[]{:T(256)} %broadcast.56), dimensions={1,2}, to_apply=%bitcast.40.reduce_sub_computation | reduce | bytes 589826
  146.0 0.9 reshape.89
  147.0 20.0 %all_to_all.8 = bf16[64,2,1152]{2,1,0:T(2,128)(2,1)S(1)} all-to-all(bf16[64,2,1152]{2,1,0:T(2,128)(2,1)S(1)} %reshape.89), channel_id=1, replica_groups=mesh['ha'=64,'ta'=4] {'ha'}, dimensions={0} | all-to-all | bytes 589824 | tf_op jit(solution)/shard_map/all_to_all | solution.py:375
  166.9 2.8 %reshape.90 = bf16[2048,1,1,72]{3,2,1,0:T(2,128)(2,1)} reshape(bf16[64,2,1152]{2,1,0:T(2,128)(2,1)S(1)} %all_to_all.8) | data formatting | bytes 589824
  169.7 1.4 copy.49
  171.7 2.8 %fusion.14 = bf16[8,32,1152]{2,1,0:T(8,128)(2,1)} fusion(f32[8,32,1152]{2,1,0:T(8,128)S(1)} %copy-done.9, bf16[8,32,576]{2,1,0:T(8,128)(2,1)S(1)} %dot_general.19, bf16[576,1152]{1,0:T(8,128)(2,1)} %param.31, f32[1152]{0:T(1024)S(1)} %copy-done.15), kind=kOutput, calls=%fused_computation.20 | convolution fusion | flops 340623360 | bytes 3396096 | tf_op jit(solution)/shard_map/dot_general | solution.py:381
  (49 shorter events, 3.9 us)
Async XLA Ops:
  0.0 44.4 %copy-start = (bf16[588,1152]{1,0:T(8,128)(2,1)S(1)}, bf16[588,1152]{1,0:T(8,128)(2,1)}, u32[]{:S(2)}) copy-start(bf16[588,1152]{1,0:T(8,128)(2,1)} %param.24) | copy-start | bytes 4064260
  1.8 1.3 copy-start.1
  3.0 0.9 copy-start.2
  3.9 0.9 copy-start.3
  4.8 0.9 copy-start.4
  5.7 0.8 copy-start.5
  6.5 0.7 copy-start.6
  7.2 0.7 copy-start.7
  7.8 36.6 %copy-start.17 = (f32[1152]{0:T(1024)S(1)}, f32[1152]{0:T(1024)}, u32[]{:S(2)}) copy-start(f32[1152]{0:T(1024)} %param.25) | copy-start | bytes 13828
  44.5 1.1 copy-start.13
  44.5 1.1 copy-start.14
  44.5 2.6 %copy-start.16 = (bf16[1152,1728]{0,1:T(8,128)(2,1)S(1)}, bf16[1152,1728]{0,1:T(8,128)(2,1)}, u32[]{:S(2)}) copy-start(bf16[1152,1728]{0,1:T(8,128)(2,1)} %param.29) | copy-start | bytes 11943940
  45.2 1.0 copy-start.8
  45.3 1.8 %copy-start.18 = (f32[1728]{0:T(1024)S(1)}, f32[1728]{0:T(1024)}, u32[]{:S(2)}) copy-start(f32[1728]{0:T(1024)} %param.30) | copy-start | bytes 20740
  56.4 39.8 %all-to-all-start = ((bf16[64,1,32,216]{3,2,1,0:T(8,128)(2,1)}), bf16[64,1,32,216]{3,2,1,0:T(8,128)(2,1)}, u32[]{:S(2)}, u32[]{:S(2)}) async-start(bf16[64,1,32,216]{3,2,1,0:T(8,128)(2,1)} %bitcast.64), calls=%async_computation | async-start | bytes 2097152 | tf_op jit(solution)/shard_map/all_to_all | solution.py:374
  106.3 3.6 %copy-start.10 = (bf16[1,2048,1,72]{3,2,1,0:T(2,128)(2,1)S(1)}, bf16[1,2048,1,72]{3,2,1,0:T(2,128)(2,1)}, u32[]{:S(2)}) copy-start(bf16[1,2048,1,72]{3,2,1,0:T(2,128)(2,1)} %get-tuple-element.68) | copy-start | bytes 884740
  108.9 1.6 copy-start.12
  114.1 1.0 copy-start.11
  119.8 1.0 copy-start.11
  125.5 1.0 copy-start.11
  131.2 1.0 copy-start.11
  169.7 2.0 %copy-start.9 = (f32[8,32,1152]{2,1,0:T(8,128)S(1)}, f32[8,32,1152]{2,1,0:T(8,128)}, u32[]{:S(2)}) copy-start(f32[8,32,1152]{2,1,0:T(8,128)} %copy-done.8) | copy-start | bytes 3538948
  169.7 2.0 %copy-start.15 = (f32[1152]{0:T(1024)S(1)}, f32[1152]{0:T(1024)}, u32[]{:S(2)}) copy-start(f32[1152]{0:T(1024)} %param.32) | copy-start | bytes 13828

commit v2 on v1

--- a/solution.py
+++ b/solution.py
@@ -301,42 +301,238 @@
     )
 
 
-import math
-
-def layer_norm(values, gain, shift_terms):
-    widened = values.astype(jnp.float32)
-    centre = jnp.mean(widened, axis=-1, keepdims=True)
-    spread = jnp.mean((widened - centre) * (widened - centre), axis=-1, keepdims=True)
-    return ((widened - centre) * lax.rsqrt(spread + 1e-06) * gain + shift_terms).astype(
-        jnp.bfloat16
-    )
-
-
-def attend(block):
-    items = block.shape[1]
-    length = block.shape[2]
-    split = block.reshape(items, length, 3, HD)
-    queries = split[:, :, 0]
-    keys_all = split[:, :, 1]
-    values_all = split[:, :, 2]
-    rows_step = math.gcd(length, 512)
-
-    def one_block(start):
-        query_rows = lax.dynamic_slice_in_dim(queries, start, rows_step, 1)
-        scores = jnp.einsum(
-            "gqd,gkd->gqk", query_rows, keys_all, preferred_element_type=jnp.float32
-        ) * HD ** (-0.5)
-        highest = jnp.max(scores, axis=-1, keepdims=True)
-        expo = jnp.exp(scores - highest)
-        weights = (expo / jnp.sum(expo, axis=-1, keepdims=True)).astype(jnp.bfloat16)
-        return jnp.einsum(
-            "gqk,gkd->gqd", weights, values_all, preferred_element_type=jnp.float32
-        ).astype(jnp.bfloat16)
-
-    starts = jnp.arange(length // rows_step, dtype=jnp.int32) * rows_step
-    pieces = lax.map(one_block, starts)
-    joined = jnp.transpose(pieces, (1, 0, 2, 3)).reshape(items, length, HD)
-    return joined[None]
+def block_kernel(
+    own_ref,
+    pos_all_ref,
+    pos_ref,
+    pw_hbm,
+    pb_hbm,
+    lng_hbm,
+    lnb_hbm,
+    wqkv_hbm,
+    bqkv_hbm,
+    wout_hbm,
+    bout_hbm,
+    out_ref,
+    pw_ref,
+    pb_ref,
+    lng_ref,
+    lnb_ref,
+    wqkv_ref,
+    bqkv_ref,
+    wout_ref,
+    bout_ref,
+    x_in,
+    resid,
+    normed,
+    q_out,
+    q_in,
+    k_all,
+    v_all,
+    c_out,
+    c_in,
+    z_out,
+    z_in,
+    load_sem,
+    send_sem,
+    recv_sem,
+):
+    s = lax.axis_index("ha")
+    t = lax.axis_index("ta")
+    z = s // 8
+    q = s % 8
+    loads = [
+        pltpu.make_async_copy(source, target, load_sem.at[at])
+        for at, (source, target) in enumerate(
+            [
+                (pw_hbm, pw_ref),
+                (pb_hbm, pb_ref),
+                (lng_hbm, lng_ref),
+                (lnb_hbm, lnb_ref),
+                (wqkv_hbm, wqkv_ref),
+                (bqkv_hbm, bqkv_ref),
+                (wout_hbm, wout_ref),
+                (bout_hbm, bout_ref),
+            ]
+        )
+    ]
+    for load in loads:
+        load.start()
+    planes = [lax.rem(z + d, 8) for d in range(1, 8)]
+    heads = [lax.rem(q + d, 8) for d in range(1, 8)]
+    column = [{"ha": plane * 8 + q, "ta": t} for plane in planes]
+    cluster = [{"ha": z * 8 + head, "ta": t} for head in heads]
+    greet(column + cluster)
+
+    frames = []
+    for d in range(7):
+        copy = remote(
+            own_ref.at[planes[d]], x_in.at[z], send_sem.at[d], recv_sem.at[d], column[d]
+        )
+        copy.start()
+        frames.append(copy)
+    x_in[z] = own_ref[z]
+
+    row = lax.broadcasted_iota(jnp.int32, (80, 256), 0)
+    for h in range(8):
+        q_out[h, 0] = jnp.zeros((80, 256), BF16)
+        q_out[h, 1] = jnp.zeros((80, 256), BF16)
+        q_out[h, 2] = jnp.where(row == HD, 1.0, 0.0).astype(BF16)
+    z_out[...] = jnp.zeros_like(z_out)
+
+    def embed(tokens, positions):
+        value = jnp.dot(
+            tokens.reshape(256, 640)[:, :588], pw_ref[...], preferred_element_type=F32
+        ).reshape(8, 32, 1152)
+        return (value + pb_ref[...].reshape(1, 1, 1152) + positions.astype(F32)).astype(BF16)
+
+    for at in (0, 1):
+        loads[at].wait()
+    resid[...] = embed(own_ref[...], pos_ref[...].reshape(1, 32, 1152)).reshape(256, 1152)
+    for at in (2, 3, 5, 4):
+        loads[at].wait()
+    bias = jnp.transpose(jnp.broadcast_to(bqkv_ref[...], (8, 1728)))[:, 0:1]
+    for copy in frames:
+        copy.wait()
+    value = embed(x_in[...], pos_all_ref[...]).reshape(256, 1152).astype(F32)
+    centre = jnp.mean(value, axis=-1, keepdims=True)
+    value = value - centre
+    spread = jnp.mean(value * value, axis=-1, keepdims=True)
+    normed[...] = (value * lax.rsqrt(spread + 1e-06) * lng_ref[...] + lnb_ref[...]).astype(BF16)
+
+    pairs = {}
+    for kind in (1, 2, 0):
+        rows = slice(kind * 576, kind * 576 + 576)
+        made = (
+            lax.dot_general(
+                wqkv_ref[rows, :], normed[...], (((1,), (1,)), ((), ())), preferred_element_type=F32
+            )
+            + bias[rows]
+        ).astype(F32)
+        for h in range(8):
+            q_out[h, kind, 0:HD] = made[h * HD : (h + 1) * HD].astype(BF16)
+        for d in range(7):
+            at = 7 + kind * 7 + d
+            copy = remote(
+                q_out.at[heads[d], kind],
+                q_in.at[q, kind],
+                send_sem.at[at],
+                recv_sem.at[at],
+                cluster[d],
+            )
+            copy.start()
+            pairs[kind, d] = copy
+        q_in[q, kind] = q_out[q, kind]
+
+    for d in range(7):
+        pairs[1, d].wait()
+    for p in range(8):
+        k_all[p * 256 : (p + 1) * 256, :] = jnp.transpose(q_in[p, 1].astype(F32)).astype(BF16)
+    for d in range(7):
+        pairs[2, d].wait()
+    for p in range(8):
+        v_all[:, p * 256 : (p + 1) * 256] = q_in[p, 2]
+    for d in range(7):
+        pairs[0, d].wait()
+
+    rate = HD ** (-0.5) * 1.4426950408889634
+
+    def attend(i, carry):
+        p = lax.rem(q + 1 + i, 8)
+        scores = jnp.dot(k_all[...], q_in[p, 0], preferred_element_type=F32)
+        highest = jnp.max(scores, axis=0, keepdims=True)
+        weights = jnp.exp2((scores - highest) * rate).astype(BF16)
+        mixed = jnp.dot(v_all[...], weights, preferred_element_type=F32)
+        c_out[p] = (mixed / mixed[HD : HD + 1]).astype(BF16)
+
+        @pl.when(i < 7)
+        def _():
+            remote(
+                c_out.at[p],
+                c_in.at[q],
+                send_sem.at[28 + i],
+                recv_sem.at[28 + i],
+                {"ha": z * 8 + p, "ta": t},
+            ).start()
+
+        return carry
+
+    lax.fori_loop(0, 8, attend, 0)
+    c_in[q] = c_out[q]
+    for d in range(7):
+        remote(
+            c_out.at[heads[d]], c_in.at[q], send_sem.at[28 + d], recv_sem.at[28 + d], cluster[d]
+        ).wait()
+    sides = jnp.concatenate([c_in[h, 0:HD].astype(F32) for h in range(8)], axis=0)
+    z_out[:, :, 0:576] = jnp.transpose(sides).astype(BF16).reshape(8, 32, 576)
+    backs = []
+    for d in range(7):
+        copy = remote(
+            z_out.at[planes[d]], z_in.at[z], send_sem.at[35 + d], recv_sem.at[35 + d], column[d]
+        )
+        copy.start()
+        backs.append(copy)
+    z_in[z] = z_out[z]
+    loads[6].wait()
+    loads[7].wait()
+    for copy in backs:
+        copy.wait()
+    result = jnp.dot(
+        z_in[...].reshape(256, 640)[:, :576], wout_ref[...], preferred_element_type=F32
+    )
+    result = result + bout_ref[...] + resid[...].astype(F32)
+    out_ref[...] = result.astype(BF16).reshape(8, 32, 1152)
+
+
+def block(own, pos_all, pos, patch_weight, patch_bias, ln_gain, ln_bias, w_qkv, b_qkv, w_out, b_out):
+    vmem = pl.BlockSpec(memory_space=pltpu.VMEM)
+    hbm = pl.BlockSpec(memory_space=pl.ANY)
+    return pl.pallas_call(
+        block_kernel,
+        out_shape=jax.ShapeDtypeStruct((8, 32, 1152), BF16),
+        in_specs=[vmem] * 3 + [hbm] * 8,
+        out_specs=vmem,
+        scratch_shapes=[
+            pltpu.VMEM((588, 1152), BF16),
+            pltpu.VMEM((1, 1152), F32),
+            pltpu.VMEM((1, 1152), F32),
+            pltpu.VMEM((1, 1152), F32),
+            pltpu.VMEM((1728, 1152), BF16),
+            pltpu.VMEM((1, 1728), F32),
+            pltpu.VMEM((576, 1152), BF16),
+            pltpu.VMEM((1, 1152), F32),
+            pltpu.VMEM((8, 32, 640), BF16),
+            pltpu.VMEM((256, 1152), BF16),
+            pltpu.VMEM((256, 1152), BF16),
+            pltpu.VMEM((8, 3, 80, 256), BF16),
+            pltpu.VMEM((8, 3, 80, 256), BF16),
+            pltpu.VMEM((2048, 80), BF16),
+            pltpu.VMEM((80, 2048), BF16),
+            pltpu.VMEM((8, 80, 256), BF16),
+            pltpu.VMEM((8, 80, 256), BF16),
+            pltpu.VMEM((8, 32, 640), BF16),
+            pltpu.VMEM((8, 32, 640), BF16),
+            pltpu.SemaphoreType.DMA((8,)),
+            pltpu.SemaphoreType.DMA((42,)),
+            pltpu.SemaphoreType.DMA((42,)),
+        ],
+        compiler_params=pltpu.CompilerParams(
+            collective_id=1, has_side_effects=True, vmem_limit_bytes=56 * 1024 * 1024
+        ),
+        name="block",
+    )(
+        own,
+        pos_all,
+        pos,
+        patch_weight,
+        patch_bias.reshape(1, -1),
+        ln_gain.reshape(1, -1),
+        ln_bias.reshape(1, -1),
+        w_qkv.T,
+        b_qkv.reshape(1, -1),
+        w_out,
+        b_out.reshape(1, -1),
+    )
 
 
 def shards(
@@ -356,33 +552,19 @@
     b_out,
 ):
     own, pos_all = patches(features, norm_gain, head_weight, head_bias, frame_order, pos_embed)
-    mine = own[:, :, :588]
-    frame_count, across, _ = mine.shape
-    embedded = jnp.dot(
-        mine.reshape(-1, mine.shape[2]), patch_weight, preferred_element_type=jnp.float32
-    ).reshape(frame_count, across, -1)
-    embedded = (embedded + patch_bias + pos_embed.astype(jnp.float32)).astype(jnp.bfloat16)
-    width = embedded.shape[2]
-    normed = layer_norm(embedded, ln_gain, ln_bias)
-    projected = (
-        jnp.dot(normed.reshape(-1, width), w_qkv, preferred_element_type=jnp.float32) + b_qkv
-    )
-    projected = projected.astype(jnp.bfloat16).reshape(frame_count, across, 3, HEADS, HD)
-    slabs = lax.axis_size("ha")
-    groups = frame_count * HEADS // slabs
-    arranged = jnp.transpose(projected, (0, 3, 1, 2, 4)).reshape(slabs, groups, across, 3 * HD)
-    context = attend(lax.all_to_all(arranged, "ha", split_axis=0, concat_axis=2, tiled=True))
-    returned = lax.all_to_all(context, "ha", split_axis=2, concat_axis=0, tiled=True)
-    merged = (
-        returned.reshape(frame_count, HEADS, across, HD)
-        .transpose(0, 2, 1, 3)
-        .reshape(-1, HEADS * HD)
-    )
-    result = jnp.dot(merged, w_out, preferred_element_type=jnp.float32).reshape(
-        frame_count, across, width
-    )
-    result = result + b_out + embedded.astype(jnp.float32)
-    return result.astype(jnp.bfloat16)
+    return block(
+        own,
+        pos_all,
+        pos_embed,
+        patch_weight,
+        patch_bias,
+        ln_gain,
+        ln_bias,
+        w_qkv,
+        b_qkv,
+        w_out,
+        b_out,
+    )
 
 
 def solution(mesh):

time: 176 us -> 108 us (0.61)
  Pallas kernels: 36.6 us -> 90.6 us
  waiting for transfers between devices: 27.9 us -> 0 us
  local copies, waits for them, and re-layouts: 39.8 us -> 16 us
  blocking collectives: 20 us -> 0 us
  other arithmetic: 17 us -> 0.68 us
  matrix products: 13.3 us -> 0 us
  starting transfers between devices: 11.9 us -> 0 us
  loops' own time: 7.74 us -> 0 us
    pallas_call x0 -> x1, Pallas kernels: none -> 55.1 us  [block(): pl.pallas_call(block_kernel, out_shape=jax.ShapeDtypeStruct((8, 32, 1152)...]
    all_to_all x1 -> x0, waiting for transfers between devices: 27.9 us -> none  [shards(): lax.all_to_all(arranged, 'ha', split_axis=0, concat_axis=2, tiled=True)]
    all_to_all x1 -> x0, blocking collectives: 20 us -> none  [shards(): lax.all_to_all(context, 'ha', split_axis=2, concat_axis=0, tiled=True)]
    dot_general x11 -> x0, matrix products: 13.3 us -> none  [the longest x4 4.54 us: one_block(): jnp.einsum('gqk,gkd->gqd', weights, values_all, preferred_element_type=jn...]
    all_to_all x1 -> x0, starting transfers between devices: 11.9 us -> none  [shards(): lax.all_to_all(arranged, 'ha', split_axis=0, concat_axis=2, tiled=True)]
    unnamed x1 -> x0, other arithmetic: 11.5 us -> none
    slice x4 -> x0, local copies, waits for them, and re-layouts: 8.8 us -> none  [the longest x2 5.92 us: attend(): values_all = split[:, :, 2]]
    another operation x1 -> x0, loops' own time: 7.74 us -> none  [attend(): pieces = lax.map(one_block, starts)]
  transfers between devices with their start and end apart: 1 -> 0, of which waited for: 1 -> 0; matrix products, arithmetic and copies ran while one was open for 0% -> 0% of each run, Pallas kernels for 0% -> 0%
where the time goes in v2:
time: 108 us; the launch traced here: 107 us
  Pallas kernels  90.6 us (84%)
  local copies, waits for them, and re-layouts  16 us (15%)
    pallas_call x1, Pallas kernels, block(): pl.pallas_call(block_kernel, out_shape=jax.ShapeDtypeStruct((8, 32, 1152)...  55.1 us
    pallas_call x1, Pallas kernels, patches(): pl.pallas_call(patches_kernel, out_shape=(jax.ShapeDtypeStruct((8, 32, 64...  35.5 us
    unnamed x19, local copies, waits for them, and re-layouts  9.5 us

profile of v2, /device:TPU:1, one launch (start us, length us, event | category | flops | bytes accessed | tf_op | source)
XLA Modules:
  0.0 107.4 jit_solution(8881797239742039468)
XLA Ops:
  0.0 0.7 broadcast_multiply_fusion
  0.7 1.3 %reshape.17.pb_hbm = f32[1,1152]{1,0:T(1,128)} reshape(f32[1152]{0:T(1024)} %param.23) | data formatting | bytes 9216 | tf_op jit(solution)/shard_map/reshape | solution.py:528
  2.0 1.3 %reshape.18.lng_hbm = f32[1,1152]{1,0:T(1,128)} reshape(f32[1152]{0:T(1024)} %param.25) | data formatting | bytes 9216 | tf_op jit(solution)/shard_map/reshape | solution.py:529
  3.3 1.3 %reshape.19.lnb_hbm = f32[1,1152]{1,0:T(1,128)} reshape(f32[1152]{0:T(1024)} %param.26) | data formatting | bytes 9216 | tf_op jit(solution)/shard_map/reshape | solution.py:530
  4.6 1.3 %reshape.21.bout_hbm = f32[1,1152]{1,0:T(1,128)} reshape(f32[1152]{0:T(1024)} %param.30) | data formatting | bytes 9216 | tf_op jit(solution)/shard_map/reshape | solution.py:534
  5.8 1.3 %reshape.20.bqkv_hbm = f32[1,1728]{1,0:T(1,128)} reshape(f32[1728]{0:T(1024)} %param.28) | data formatting | bytes 13824 | tf_op jit(solution)/shard_map/reshape | solution.py:532
  7.1 0.1 broadcast_in_dim.2.gain_ref
  7.2 0.0 copy-start
  7.2 1.2 %copy-done = bf16[896,640]{1,0:T(8,128)(2,1)S(1)} copy-done((bf16[896,640]{1,0:T(8,128)(2,1)S(1)}, bf16[896,640]{1,0:T(8,128)(2,1)}, u32[]{:S(2)}) %copy-start) | copy-done | bytes 1146904
  8.5 0.0 copy-start.3
  8.5 0.9 copy-done.3
  9.4 0.0 copy-start.4
  9.4 0.9 copy-done.4
  10.3 0.0 copy-start.5
  10.3 0.9 copy-done.5
  11.2 0.0 copy-start.6
  11.2 0.8 copy-done.6
  12.0 0.0 copy-start.7
  12.0 0.7 copy-done.7
  12.6 0.0 copy-start.8
  12.6 0.7 copy-done.8
  13.3 35.5 %patches.1 = (bf16[8,32,640]{2,1,0:T(8,128)(2,1)S(1)}, bf16[8,32,1152]{2,1,0:T(8,128)(2,1)S(1)}) custom-call(bf16[8,7,192,224]{3,2,1,0:T(8,128)(2,1)} %bitcast.4, bf16[3,27,192]{2,1,0:T(8,128)(2,1)S(1)} %bitcast.3, f32[192,224]{1,0:T(8,128)S(1)} %broadcast_in_dim.2.gain_ref, f32[3]{0:T(128)S(1)} %copy-done.7, s32[32]{0:T(128)S(1)} %copy-done.8, ...), custom_call_target="tpu_custom_call" | custom-call | tf_op jit(solution)/shard_map/patches/pallas_call | solution.py:260
  48.8 0.0 copy-start.1
  48.8 0.8 copy-done.1
  49.6 0.0 copy-start.2
  49.6 0.7 copy-done.2
  50.3 55.1 %block.1 = bf16[8,32,1152]{2,1,0:T(8,128)(2,1)} custom-call(bf16[8,32,640]{2,1,0:T(8,128)(2,1)} %copy-done.2, bf16[8,32,1152]{2,1,0:T(8,128)(2,1)} %copy-done.1, bf16[32,1152]{1,0:T(8,128)(2,1)} %pos_ref.3, bf16[588,1152]{1,0:T(8,128)(2,1)} %pw_hbm.1, f32[1,1152]{1,0:T(1,128)} %reshape.17.pb_hbm, f32[1,1152]{1,0:T(1,128)} %reshape.18.lng_hbm, ...), custom_call_target="tpu_custom_call" | custom-call | tf_op jit(solution)/shard_map/block/pallas_call | solution.py:490
  105.4 1.9 %copy.19 = bf16[8,32,1152]{2,1,0:T(8,128)(2,1)} copy(bf16[8,32,1152]{2,1,0:T(8,128)(2,1)} %block.1) | data formatting | bytes 1179648
Async XLA Ops:
  7.2 1.3 %copy-start = (bf16[896,640]{1,0:T(8,128)(2,1)S(1)}, bf16[896,640]{1,0:T(8,128)(2,1)}, u32[]{:S(2)}) copy-start(bf16[896,640]{1,0:T(8,128)(2,1)} %constant.10.clone.place_ref) | copy-start | bytes 3440644
  8.5 0.9 copy-start.3
  9.4 0.9 copy-start.4
  10.3 0.9 copy-start.5
  11.2 0.8 copy-start.6
  12.0 0.7 copy-start.7
  12.6 0.7 copy-start.8
  48.8 0.8 copy-start.1
  49.6 0.7 copy-start.2

commit v3 on v2

--- a/solution.py
+++ b/solution.py
@@ -66,8 +66,26 @@
     )
 
 
-def patches_kernel(
+def kernel(
     x_hbm,
+    taps_hbm,
+    gain_hbm,
+    bias_hbm,
+    order_hbm,
+    combine_hbm,
+    column_hbm,
+    place_hbm,
+    pos_hbm,
+    pw_hbm,
+    pb_hbm,
+    lng_hbm,
+    lnb_hbm,
+    wqkv_hbm,
+    bqkv_hbm,
+    wout_hbm,
+    bout_hbm,
+    out_ref,
+    x_ref,
     taps_ref,
     gain_ref,
     bias_ref,
@@ -76,9 +94,14 @@
     column_ref,
     place_ref,
     pos_ref,
-    own_ref,
-    pos_all_ref,
-    x_ref,
+    pw_ref,
+    pb_ref,
+    lng_ref,
+    lnb_ref,
+    wqkv_ref,
+    bqkv_ref,
+    wout_ref,
+    bout_ref,
     w_ref,
     acc,
     vs,
@@ -92,7 +115,26 @@
     grid,
     gathered,
     pos_in,
+    own_ref,
+    x_in,
+    resid,
+    normed,
+    q_out,
+    q_in,
+    k_all,
+    v_all,
+    c_out,
+    c_in,
+    z_out,
+    z_in,
     x_sem,
+    load_sem,
+    near_send,
+    near_recv,
+    ring_send,
+    ring_recv,
+    pos_send,
+    pos_recv,
     send_sem,
     recv_sem,
 ):
@@ -105,12 +147,63 @@
     after = lax.rem(t + 1, 4)
     prior = lax.rem(t + 3, 4)
 
-    loads = [pltpu.make_async_copy(x_hbm.at[f], x_ref.at[f], x_sem.at[f]) for f in range(8)]
+    names = [
+        "taps",
+        "gain",
+        "bias",
+        "order",
+        "combine",
+        "column",
+        "place",
+        "pos",
+        "pw",
+        "pb",
+        "lng",
+        "lnb",
+        "wqkv",
+        "bqkv",
+        "wout",
+        "bout",
+    ]
+    sources = [
+        (taps_hbm, taps_ref),
+        (gain_hbm, gain_ref),
+        (bias_hbm, bias_ref),
+        (order_hbm, order_ref),
+        (combine_hbm, combine_ref),
+        (column_hbm, column_ref),
+        (place_hbm, place_ref),
+        (pos_hbm, pos_ref),
+        (pw_hbm, pw_ref),
+        (pb_hbm, pb_ref),
+        (lng_hbm, lng_ref),
+        (lnb_hbm, lnb_ref),
+        (wqkv_hbm, wqkv_ref),
+        (bqkv_hbm, bqkv_ref),
+        (wout_hbm, wout_ref),
+        (bout_hbm, bout_ref),
+    ]
+    loads = {
+        name: pltpu.make_async_copy(source, target, load_sem.at[at])
+        for at, (name, (source, target)) in enumerate(zip(names, sources))
+    }
+
+    def ready(*wanted):
+        for name in wanted:
+            loads.pop(name).wait()
+
+    loads["taps"].start()
+    loads["gain"].start()
     for f in [6, 7, 0, 1, 2, 3, 4, 5]:
-        loads[f].start()
-
+        pltpu.make_async_copy(x_hbm.at[f], x_ref.at[f], x_sem.at[f]).start()
+    for name in names[2:]:
+        loads[name].start()
+
+    planes = [lax.rem(z + d, 8) for d in range(1, 8)]
+    heads = [lax.rem(q + d, 8) for d in range(1, 8)]
     ring = [{"ha": s, "ta": lax.rem(t + d, 4)} for d in range(1, 4)]
-    column = [{"ha": lax.rem(z + d, 8) * 8 + q, "ta": t} for d in range(1, 8)]
+    column = [{"ha": plane * 8 + q, "ta": t} for plane in planes]
+    cluster = [{"ha": z * 8 + head, "ta": t} for head in heads]
     near = [
         {"ha": below, "ta": t},
         {"ha": above, "ta": t},
@@ -119,25 +212,20 @@
         {"ha": below, "ta": prior},
         {"ha": above, "ta": prior},
     ]
-    greet(ring + column + near)
-
-    pos_copies = []
-    for d in range(7):
-        copy = remote(pos_ref, pos_in.at[z], send_sem.at[8 + d], recv_sem.at[8 + d], column[d])
-        copy.start()
-        pos_copies.append(copy)
 
     w_ref[...] = jnp.zeros_like(w_ref)
+    ready("taps", "gain")
     for tap in range(3):
         w_ref[tap, 0:27, :] = taps_ref[tap].astype(F32)
     acc[...] = jnp.zeros_like(acc)
+    gain = jnp.transpose(jnp.broadcast_to(0.5 * gain_ref[...].reshape(1, 192), (8, 192)))[:, 0:1]
     weight = w_ref[...].reshape(96, 192).astype(BF16)
 
     def convolve(f):
         for r in range(7):
             x = x_ref[f, r].astype(F32)
             factor = lax.rsqrt(jnp.sum(x * x, axis=0, keepdims=True) * (1.0 / 192.0) + 1e-06)
-            u = x * factor * gain_ref[...]
+            u = x * factor * gain
             a = (u + u * jnp.tanh(u)).astype(BF16)
             res = jnp.dot(weight, a, preferred_element_type=F32)
             rows = pl.ds(r * 32, 32)
@@ -171,17 +259,25 @@
         convolve(f)
         return carry
 
+    greet(ring + column + cluster + near)
+    ready("pos")
+    pos_copies = []
+    for d in range(7):
+        copy = remote(pos_ref, pos_in.at[z], pos_send.at[d], pos_recv.at[d], column[d])
+        copy.start()
+        pos_copies.append(copy)
     lax.fori_loop(0, 2, late, 0)
+    ready("combine")
     for f in (8, 9):
         combine(f)
     tail = pl.ds(8, 2)
     body = pl.ds(0, 8)
     halo = [
-        remote(vs.at[tail], vin, send_sem.at[0], recv_sem.at[0], {"ha": s, "ta": after}),
-        remote(edn.at[tail], edn_c, send_sem.at[1], recv_sem.at[1], near[2]),
-        remote(eup.at[tail], eup_c, send_sem.at[2], recv_sem.at[2], near[3]),
-        remote(edn.at[body], edn_in, send_sem.at[3], recv_sem.at[3], near[0]),
-        remote(eup.at[body], eup_in, send_sem.at[4], recv_sem.at[4], near[1]),
+        remote(vs.at[tail], vin, near_send.at[0], near_recv.at[0], {"ha": s, "ta": after}),
+        remote(edn.at[tail], edn_c, near_send.at[1], near_recv.at[1], near[2]),
+        remote(eup.at[tail], eup_c, near_send.at[2], near_recv.at[2], near[3]),
+        remote(edn.at[body], edn_in, near_send.at[3], near_recv.at[3], near[0]),
+        remote(eup.at[body], eup_in, near_send.at[4], near_recv.at[4], near[1]),
     ]
     for copy in halo[:3]:
         copy.start()
@@ -195,6 +291,7 @@
     for copy in halo[3:]:
         copy.start()
 
+    ready("bias", "order", "column", "place")
     colour = lax.rem(lax.broadcasted_iota(jnp.int32, (48, 256), 0), 3)
     bias = jnp.where(colour == 0, bias_ref[0], jnp.where(colour == 1, bias_ref[1], bias_ref[2]))
     from_above = s > 0
@@ -237,132 +334,14 @@
     copies = []
     for d in range(3):
         copy = remote(
-            gathered.at[mine], gathered.at[mine], send_sem.at[5 + d], recv_sem.at[5 + d], ring[d]
+            gathered.at[mine], gathered.at[mine], ring_send.at[d], ring_recv.at[d], ring[d]
         )
         copy.start()
         copies.append(copy)
-    for copy in pos_copies:
-        copy.wait()
-    pos_in[z] = pos_ref[...]
-    pos_all_ref[...] = pos_in[...]
     for copy in copies:
         copy.wait()
     for j in range(8):
         own_ref[j] = gathered[order_ref[t * 8 + j]]
-
-
-def patches(features, norm_gain, head_weight, head_bias, frame_order, pos_embed):
-    x = jnp.transpose(features, (0, 1, 3, 2))
-    taps = jnp.transpose(head_weight, (0, 2, 1))
-    gain = jnp.broadcast_to(0.5 * norm_gain[:, None], (192, 224))
-    vmem = pl.BlockSpec(memory_space=pltpu.VMEM)
-    smem = pl.BlockSpec(memory_space=pltpu.SMEM)
-    return pl.pallas_call(
-        patches_kernel,
-        out_shape=(
-            jax.ShapeDtypeStruct((8, 32, 640), BF16),
-            jax.ShapeDtypeStruct((8, 32, 1152), BF16),
-        ),
-        in_specs=[pl.BlockSpec(memory_space=pl.ANY), vmem, vmem, smem, smem, vmem, vmem, vmem, vmem],
-        out_specs=(vmem, vmem),
-        scratch_shapes=[
-            pltpu.VMEM((8, 7, 192, 224), BF16),
-            pltpu.VMEM((3, 32, 192), F32),
-            pltpu.VMEM((10, 224, 256), F32),
-            pltpu.VMEM((10, 2, 48, 256), F32),
-            pltpu.VMEM((10, 2, 8, 256), F32),
-            pltpu.VMEM((10, 2, 8, 256), F32),
-            pltpu.VMEM((2, 2, 48, 256), F32),
-            pltpu.VMEM((2, 2, 8, 256), F32),
-            pltpu.VMEM((2, 2, 8, 256), F32),
-            pltpu.VMEM((8, 2, 8, 256), F32),
-            pltpu.VMEM((8, 2, 8, 256), F32),
-            pltpu.VMEM((256, 896), BF16),
-            pltpu.VMEM((32, 32, 640), BF16),
-            pltpu.VMEM((8, 32, 1152), BF16),
-            pltpu.SemaphoreType.DMA((8,)),
-            pltpu.SemaphoreType.DMA((15,)),
-            pltpu.SemaphoreType.DMA((15,)),
-        ],
-        compiler_params=pltpu.CompilerParams(
-            collective_id=0, has_side_effects=True, vmem_limit_bytes=48 * 1024 * 1024
-        ),
-        name="patches",
-    )(
-        x,
-        taps,
-        gain,
-        head_bias,
-        frame_order,
-        combine_matrix(),
-        column_matrix(),
-        place_matrix(),
-        pos_embed,
-    )
-
-
-def block_kernel(
-    own_ref,
-    pos_all_ref,
-    pos_ref,
-    pw_hbm,
-    pb_hbm,
-    lng_hbm,
-    lnb_hbm,
-    wqkv_hbm,
-    bqkv_hbm,
-    wout_hbm,
-    bout_hbm,
-    out_ref,
-    pw_ref,
-    pb_ref,
-    lng_ref,
-    lnb_ref,
-    wqkv_ref,
-    bqkv_ref,
-    wout_ref,
-    bout_ref,
-    x_in,
-    resid,
-    normed,
-    q_out,
-    q_in,
-    k_all,
-    v_all,
-    c_out,
-    c_in,
-    z_out,
-    z_in,
-    load_sem,
-    send_sem,
-    recv_sem,
-):
-    s = lax.axis_index("ha")
-    t = lax.axis_index("ta")
-    z = s // 8
-    q = s % 8
-    loads = [
-        pltpu.make_async_copy(source, target, load_sem.at[at])
-        for at, (source, target) in enumerate(
-            [
-                (pw_hbm, pw_ref),
-                (pb_hbm, pb_ref),
-                (lng_hbm, lng_ref),
-                (lnb_hbm, lnb_ref),
-                (wqkv_hbm, wqkv_ref),
-                (bqkv_hbm, bqkv_ref),
-                (wout_hbm, wout_ref),
-                (bout_hbm, bout_ref),
-            ]
-        )
-    ]
-    for load in loads:
-        load.start()
-    planes = [lax.rem(z + d, 8) for d in range(1, 8)]
-    heads = [lax.rem(q + d, 8) for d in range(1, 8)]
-    column = [{"ha": plane * 8 + q, "ta": t} for plane in planes]
-    cluster = [{"ha": z * 8 + head, "ta": t} for head in heads]
-    greet(column + cluster)
 
     frames = []
     for d in range(7):
@@ -386,19 +365,20 @@
         ).reshape(8, 32, 1152)
         return (value + pb_ref[...].reshape(1, 1, 1152) + positions.astype(F32)).astype(BF16)
 
-    for at in (0, 1):
-        loads[at].wait()
+    ready("pw", "pb")
     resid[...] = embed(own_ref[...], pos_ref[...].reshape(1, 32, 1152)).reshape(256, 1152)
-    for at in (2, 3, 5, 4):
-        loads[at].wait()
-    bias = jnp.transpose(jnp.broadcast_to(bqkv_ref[...], (8, 1728)))[:, 0:1]
+    ready("lng", "lnb", "bqkv", "wqkv")
+    bias = jnp.transpose(jnp.broadcast_to(bqkv_ref[...].reshape(1, 1728), (8, 1728)))[:, 0:1]
     for copy in frames:
         copy.wait()
-    value = embed(x_in[...], pos_all_ref[...]).reshape(256, 1152).astype(F32)
+    for copy in pos_copies:
+        copy.wait()
+    pos_in[z] = pos_ref[...]
+    value = embed(x_in[...], pos_in[...]).reshape(256, 1152).astype(F32)
     centre = jnp.mean(value, axis=-1, keepdims=True)
     value = value - centre
     spread = jnp.mean(value * value, axis=-1, keepdims=True)
-    normed[...] = (value * lax.rsqrt(spread + 1e-06) * lng_ref[...] + lnb_ref[...]).astype(BF16)
+    normed[...] = (value * lax.rsqrt(spread + 1e-06) * lng_ref[...].reshape(1, 1152) + lnb_ref[...].reshape(1, 1152)).astype(BF16)
 
     pairs = {}
     for kind in (1, 2, 0):
@@ -473,66 +453,14 @@
         copy.start()
         backs.append(copy)
     z_in[z] = z_out[z]
-    loads[6].wait()
-    loads[7].wait()
+    ready("wout", "bout")
     for copy in backs:
         copy.wait()
     result = jnp.dot(
         z_in[...].reshape(256, 640)[:, :576], wout_ref[...], preferred_element_type=F32
     )
-    result = result + bout_ref[...] + resid[...].astype(F32)
+    result = result + bout_ref[...].reshape(1, 1152) + resid[...].astype(F32)
     out_ref[...] = result.astype(BF16).reshape(8, 32, 1152)
-
-
-def block(own, pos_all, pos, patch_weight, patch_bias, ln_gain, ln_bias, w_qkv, b_qkv, w_out, b_out):
-    vmem = pl.BlockSpec(memory_space=pltpu.VMEM)
-    hbm = pl.BlockSpec(memory_space=pl.ANY)
-    return pl.pallas_call(
-        block_kernel,
-        out_shape=jax.ShapeDtypeStruct((8, 32, 1152), BF16),
-        in_specs=[vmem] * 3 + [hbm] * 8,
-        out_specs=vmem,
-        scratch_shapes=[
-            pltpu.VMEM((588, 1152), BF16),
-            pltpu.VMEM((1, 1152), F32),
-            pltpu.VMEM((1, 1152), F32),
-            pltpu.VMEM((1, 1152), F32),
-            pltpu.VMEM((1728, 1152), BF16),
-            pltpu.VMEM((1, 1728), F32),
-            pltpu.VMEM((576, 1152), BF16),
-            pltpu.VMEM((1, 1152), F32),
-            pltpu.VMEM((8, 32, 640), BF16),
-            pltpu.VMEM((256, 1152), BF16),
-            pltpu.VMEM((256, 1152), BF16),
-            pltpu.VMEM((8, 3, 80, 256), BF16),
-            pltpu.VMEM((8, 3, 80, 256), BF16),
-            pltpu.VMEM((2048, 80), BF16),
-            pltpu.VMEM((80, 2048), BF16),
-            pltpu.VMEM((8, 80, 256), BF16),
-            pltpu.VMEM((8, 80, 256), BF16),
-            pltpu.VMEM((8, 32, 640), BF16),
-            pltpu.VMEM((8, 32, 640), BF16),
-            pltpu.SemaphoreType.DMA((8,)),
-            pltpu.SemaphoreType.DMA((42,)),
-            pltpu.SemaphoreType.DMA((42,)),
-        ],
-        compiler_params=pltpu.CompilerParams(
-            collective_id=1, has_side_effects=True, vmem_limit_bytes=56 * 1024 * 1024
-        ),
-        name="block",
-    )(
-        own,
-        pos_all,
-        pos,
-        patch_weight,
-        patch_bias.reshape(1, -1),
-        ln_gain.reshape(1, -1),
-        ln_bias.reshape(1, -1),
-        w_qkv.T,
-        b_qkv.reshape(1, -1),
-        w_out,
-        b_out.reshape(1, -1),
-    )
 
 
 def shards(
@@ -551,16 +479,86 @@
     w_out,
     b_out,
 ):
-    own, pos_all = patches(features, norm_gain, head_weight, head_bias, frame_order, pos_embed)
-    return block(
-        own,
-        pos_all,
+    hbm = pl.BlockSpec(memory_space=pl.ANY)
+    vmem = pl.BlockSpec(memory_space=pltpu.VMEM)
+    return pl.pallas_call(
+        kernel,
+        out_shape=jax.ShapeDtypeStruct((8, 32, 1152), BF16),
+        in_specs=[hbm] * 17,
+        out_specs=vmem,
+        scratch_shapes=[
+            pltpu.VMEM((8, 7, 192, 224), BF16),
+            pltpu.VMEM((3, 27, 192), BF16),
+            pltpu.VMEM((192,), F32),
+            pltpu.SMEM((3,), F32),
+            pltpu.SMEM((32,), jnp.int32),
+            pltpu.VMEM((256, 224), BF16),
+            pltpu.VMEM((224, 256), BF16),
+            pltpu.VMEM((896, 640), BF16),
+            pltpu.VMEM((32, 1152), BF16),
+            pltpu.VMEM((588, 1152), BF16),
+            pltpu.VMEM((1152,), F32),
+            pltpu.VMEM((1152,), F32),
+            pltpu.VMEM((1152,), F32),
+            pltpu.VMEM((1728, 1152), BF16),
+            pltpu.VMEM((1728,), F32),
+            pltpu.VMEM((576, 1152), BF16),
+            pltpu.VMEM((1152,), F32),
+            pltpu.VMEM((3, 32, 192), F32),
+            pltpu.VMEM((10, 224, 256), F32),
+            pltpu.VMEM((10, 2, 48, 256), F32),
+            pltpu.VMEM((10, 2, 8, 256), F32),
+            pltpu.VMEM((10, 2, 8, 256), F32),
+            pltpu.VMEM((2, 2, 48, 256), F32),
+            pltpu.VMEM((2, 2, 8, 256), F32),
+            pltpu.VMEM((2, 2, 8, 256), F32),
+            pltpu.VMEM((8, 2, 8, 256), F32),
+            pltpu.VMEM((8, 2, 8, 256), F32),
+            pltpu.VMEM((256, 896), BF16),
+            pltpu.VMEM((32, 32, 640), BF16),
+            pltpu.VMEM((8, 32, 1152), BF16),
+            pltpu.VMEM((8, 32, 640), BF16),
+            pltpu.VMEM((8, 32, 640), BF16),
+            pltpu.VMEM((256, 1152), BF16),
+            pltpu.VMEM((256, 1152), BF16),
+            pltpu.VMEM((8, 3, 80, 256), BF16),
+            pltpu.VMEM((8, 3, 80, 256), BF16),
+            pltpu.VMEM((2048, 80), BF16),
+            pltpu.VMEM((80, 2048), BF16),
+            pltpu.VMEM((8, 80, 256), BF16),
+            pltpu.VMEM((8, 80, 256), BF16),
+            pltpu.VMEM((8, 32, 640), BF16),
+            pltpu.VMEM((8, 32, 640), BF16),
+            pltpu.SemaphoreType.DMA((8,)),
+            pltpu.SemaphoreType.DMA((16,)),
+            pltpu.SemaphoreType.DMA((5,)),
+            pltpu.SemaphoreType.DMA((5,)),
+            pltpu.SemaphoreType.DMA((3,)),
+            pltpu.SemaphoreType.DMA((3,)),
+            pltpu.SemaphoreType.DMA((7,)),
+            pltpu.SemaphoreType.DMA((7,)),
+            pltpu.SemaphoreType.DMA((42,)),
+            pltpu.SemaphoreType.DMA((42,)),
+        ],
+        compiler_params=pltpu.CompilerParams(
+            collective_id=0, has_side_effects=True, vmem_limit_bytes=60 * 1024 * 1024
+        ),
+        name="decoder_block",
+    )(
+        jnp.transpose(features, (0, 1, 3, 2)),
+        jnp.transpose(head_weight, (0, 2, 1)),
+        norm_gain,
+        head_bias,
+        frame_order,
+        combine_matrix(),
+        column_matrix(),
+        place_matrix(),
         pos_embed,
         patch_weight,
         patch_bias,
         ln_gain,
         ln_bias,
-        w_qkv,
+        w_qkv.T,
         b_qkv,
         w_out,
         b_out,

time: 108 us -> 89.7 us (0.83)
  local copies, waits for them, and re-layouts: 16 us -> 1.92 us
  Pallas kernels: 90.6 us -> 87 us
    unnamed x19 -> x1, local copies, waits for them, and re-layouts: 9.5 us -> 1.92 us
    reshape x5 -> x0, local copies, waits for them, and re-layouts: 6.46 us -> none  [the longest x1 1.29 us: block(): ln_bias.reshape(1, -1)]
    pallas_call x2 -> x1, Pallas kernels: 90.6 us -> 87 us  [shards(): pl.pallas_call(kernel, out_shape=jax.ShapeDtypeStruct((8, 32, 1152), BF16...]
where the time goes in v3:
time: 89.7 us; the launch traced here: 88.9 us
  Pallas kernels  87 us (97%)
  local copies, waits for them, and re-layouts  1.92 us (2%)
    pallas_call x1, Pallas kernels, shards(): pl.pallas_call(kernel, out_shape=jax.ShapeDtypeStruct((8, 32, 1152), BF16...  87 us
    unnamed x1, local copies, waits for them, and re-layouts  1.92 us

profile of v3, /device:TPU:1, one launch (start us, length us, event | category | flops | bytes accessed | tf_op | source)
XLA Modules:
  0.0 88.9 jit_solution(10814405972339578785)
XLA Ops:
  0.0 87.0 %decoder_block.1 = bf16[8,32,1152]{2,1,0:T(8,128)(2,1)} custom-call(bf16[8,7,192,224]{3,2,1,0:T(8,128)(2,1)} %bitcast.3, bf16[3,27,192]{2,1,0:T(8,128)(2,1)} %bitcast.5, f32[192]{0:T(256)} %gain_hbm.1, f32[3]{0:T(128)} %bias_hbm.1, s32[32]{0:T(128)} %order_hbm.1, bf16[256,224]{1,0:T(8,128)(2,1)} %constant.6.clone.combine_hbm, ...), custom_call_target="tpu_custom_call" | custom-call | tf_op jit(solution)/shard_map/decoder_block/pallas_call | solution.py:484
  87.0 1.9 %copy.19 = bf16[8,32,1152]{2,1,0:T(8,128)(2,1)} copy(bf16[8,32,1152]{2,1,0:T(8,128)(2,1)} %decoder_block.1) | data formatting | bytes 1179648

commit v4 on v3

--- a/solution.py
+++ b/solution.py
@@ -43,21 +43,13 @@
     return m.astype(jnp.bfloat16)
 
 
-def place_matrix():
-    m = np.zeros((896, 640), np.float32)
-    for x in range(7):
-        for g in range(2):
-            for at, p in enumerate(P_ORDER):
-                for c in range(3):
-                    m[x * 128 + g * 64 + at * 3 + c, 3 * (14 * p + 2 * x + g) + c] = 1
+def order_matrix():
+    m = np.zeros((640, 588), np.float32)
+    for q in range(14):
+        for at, p in enumerate(P_ORDER):
+            for c in range(3):
+                m[q * 42 + at * 3 + c, 3 * (14 * p + q) + c] = 1
     return m.astype(jnp.bfloat16)
-
-
-def greet(peers):
-    barrier = pltpu.get_barrier_semaphore()
-    for peer in peers:
-        pl.semaphore_signal(barrier, inc=1, device_id=peer, device_id_type=MESH)
-    pl.semaphore_wait(barrier, len(peers))
 
 
 def remote(src, dst, send, recv, peer):
@@ -74,7 +66,7 @@
     order_hbm,
     combine_hbm,
     column_hbm,
-    place_hbm,
+    perm_hbm,
     pos_hbm,
     pw_hbm,
     pb_hbm,
@@ -92,7 +84,7 @@
     order_ref,
     combine_ref,
     column_ref,
-    place_ref,
+    perm_ref,
     pos_ref,
     pw_ref,
     pb_ref,
@@ -112,7 +104,7 @@
     eup_c,
     edn_in,
     eup_in,
-    grid,
+    pw_all,
     gathered,
     pos_in,
     own_ref,
@@ -131,6 +123,8 @@
     load_sem,
     near_send,
     near_recv,
+    edge_send,
+    edge_recv,
     ring_send,
     ring_recv,
     pos_send,
@@ -154,7 +148,7 @@
         "order",
         "combine",
         "column",
-        "place",
+        "perm",
         "pos",
         "pw",
         "pb",
@@ -172,7 +166,7 @@
         (order_hbm, order_ref),
         (combine_hbm, combine_ref),
         (column_hbm, column_ref),
-        (place_hbm, place_ref),
+        (perm_hbm, perm_ref),
         (pos_hbm, pos_ref),
         (pw_hbm, pw_ref),
         (pb_hbm, pb_ref),
@@ -213,6 +207,11 @@
         {"ha": above, "ta": prior},
     ]
 
+    peers = ring + column + cluster + near
+    barrier = pltpu.get_barrier_semaphore()
+    for peer in peers:
+        pl.semaphore_signal(barrier, inc=1, device_id=peer, device_id_type=MESH)
+
     w_ref[...] = jnp.zeros_like(w_ref)
     ready("taps", "gain")
     for tap in range(3):
@@ -254,60 +253,34 @@
         convolve(f)
         return carry
 
-    def early(f, carry):
-        pltpu.make_async_copy(x_hbm.at[f], x_ref.at[f], x_sem.at[f]).wait()
-        convolve(f)
-        return carry
-
-    greet(ring + column + cluster + near)
-    ready("pos")
-    pos_copies = []
-    for d in range(7):
-        copy = remote(pos_ref, pos_in.at[z], pos_send.at[d], pos_recv.at[d], column[d])
-        copy.start()
-        pos_copies.append(copy)
-    lax.fori_loop(0, 2, late, 0)
-    ready("combine")
-    for f in (8, 9):
-        combine(f)
-    tail = pl.ds(8, 2)
-    body = pl.ds(0, 8)
-    halo = [
-        remote(vs.at[tail], vin, near_send.at[0], near_recv.at[0], {"ha": s, "ta": after}),
-        remote(edn.at[tail], edn_c, near_send.at[1], near_recv.at[1], near[2]),
-        remote(eup.at[tail], eup_c, near_send.at[2], near_recv.at[2], near[3]),
-        remote(edn.at[body], edn_in, near_send.at[3], near_recv.at[3], near[0]),
-        remote(eup.at[body], eup_in, near_send.at[4], near_recv.at[4], near[1]),
-    ]
-    for copy in halo[:3]:
-        copy.start()
-    lax.fori_loop(0, 6, early, 0)
-
-    def combine_one(f, carry):
-        combine(f)
-        return carry
-
-    lax.fori_loop(0, 8, combine_one, 0)
-    for copy in halo[3:]:
-        copy.start()
-
-    ready("bias", "order", "column", "place")
     colour = lax.rem(lax.broadcasted_iota(jnp.int32, (48, 256), 0), 3)
-    bias = jnp.where(colour == 0, bias_ref[0], jnp.where(colour == 1, bias_ref[1], bias_ref[2]))
     from_above = s > 0
     from_below = s < 63
     from_prior = t > 0
-    for copy in halo:
-        copy.wait()
-
-    for f in range(2):
-        for g in range(2):
-            vs[f, g] += jnp.where(from_prior, vin[f, g], 0.0)
-            vs[f, g, 0:8] += jnp.where(from_prior & from_above, edn_c[f, g], 0.0) + jnp.where(
-                from_prior & from_below, eup_c[f, g], 0.0
+
+    def edges(f):
+        return [
+            remote(edn.at[f], edn_in.at[f], edge_send.at[0, f], edge_recv.at[0, f], near[0]),
+            remote(eup.at[f], eup_in.at[f], edge_send.at[1, f], edge_recv.at[1, f], near[1]),
+        ]
+
+    def spread(f):
+        slot = t * 8 + f
+        return [
+            remote(
+                gathered.at[slot],
+                gathered.at[slot],
+                ring_send.at[d, f],
+                ring_recv.at[d, f],
+                ring[d],
             )
-
-    def pixels(f, carry):
+            for d in range(3)
+        ]
+
+    def finish(f):
+        for copy in edges(f):
+            copy.wait()
+        bias = jnp.where(colour == 0, bias_ref[0], jnp.where(colour == 1, bias_ref[1], bias_ref[2]))
         parts = []
         for g in range(2):
             edge = jnp.where(from_above, edn_in[f, g], 0.0) + jnp.where(
@@ -318,28 +291,72 @@
         v = jnp.concatenate(parts, axis=0).astype(BF16)
         cols = lax.dot_general(
             column_ref[...], v, (((1,), (1,)), ((), ())), preferred_element_type=F32
-        ).astype(BF16)
-        rows = pl.ds(pl.multiple_of(f * 32, 32), 32)
-        for x in range(7):
-            grid[rows, x * 128 : (x + 1) * 128] = cols[x * 32 : (x + 1) * 32]
+        )
+        pieces = [
+            cols[x * 32 : (x + 1) * 32, g * 64 : g * 64 + 42] for x in range(7) for g in range(2)
+        ]
+        pieces.append(jnp.zeros((32, 52), F32))
+        gathered[t * 8 + f] = jnp.concatenate(pieces, axis=1).astype(BF16)
+        for copy in spread(f):
+            copy.start()
+
+    lax.fori_loop(0, 2, late, 0)
+    pl.semaphore_wait(barrier, len(peers))
+    ready("combine")
+    for f in (8, 9):
+        combine(f)
+    tail = pl.ds(8, 2)
+    halo = [
+        remote(vs.at[tail], vin, near_send.at[0], near_recv.at[0], {"ha": s, "ta": after}),
+        remote(edn.at[tail], edn_c, near_send.at[1], near_recv.at[1], near[2]),
+        remote(eup.at[tail], eup_c, near_send.at[2], near_recv.at[2], near[3]),
+    ]
+    for copy in halo:
+        copy.start()
+    ready("pos", "bias", "column")
+    pos_copies = []
+    for d in range(7):
+        copy = remote(pos_ref, pos_in.at[z], pos_send.at[d], pos_recv.at[d], column[d])
+        copy.start()
+        pos_copies.append(copy)
+
+    def early(f, carry):
+        pltpu.make_async_copy(x_hbm.at[f], x_ref.at[f], x_sem.at[f]).wait()
+        convolve(f)
+        combine(f)
+        for copy in edges(f):
+            copy.start()
+
+        @pl.when(f == 1)
+        def _():
+            for copy in halo:
+                copy.wait()
+            for first in range(2):
+                for g in range(2):
+                    extra = jnp.where(from_prior, vin[first, g], 0.0)
+                    corner = jnp.where(from_prior & from_above, edn_c[first, g], 0.0) + jnp.where(
+                        from_prior & from_below, eup_c[first, g], 0.0
+                    )
+                    vs[first, g] += extra
+                    vs[first, g, 0:8] += corner
+
+        @pl.when(f > 0)
+        def _():
+            finish(f - 1)
+
         return carry
 
-    lax.fori_loop(0, 8, pixels, 0)
-    mine = pl.ds(t * 8, 8)
-    gathered[mine] = (
-        jnp.dot(grid[...], place_ref[...], preferred_element_type=F32)
-        .astype(BF16)
-        .reshape(8, 32, 640)
-    )
-    copies = []
-    for d in range(3):
-        copy = remote(
-            gathered.at[mine], gathered.at[mine], ring_send.at[d], ring_recv.at[d], ring[d]
-        )
-        copy.start()
-        copies.append(copy)
-    for copy in copies:
-        copy.wait()
+    lax.fori_loop(0, 6, early, 0)
+    for f in (6, 7):
+        combine(f)
+        for copy in edges(f):
+            copy.start()
+    lax.fori_loop(5, 8, lambda f, carry: (finish(f), carry)[1], 0)
+    ready("perm", "pw", "order")
+    pw_all[...] = jnp.dot(perm_ref[...], pw_ref[...], preferred_element_type=F32).astype(BF16)
+    for f in range(8):
+        for copy in spread(f):
+            copy.wait()
     for j in range(8):
         own_ref[j] = gathered[order_ref[t * 8 + j]]
 
@@ -361,11 +378,11 @@
 
     def embed(tokens, positions):
         value = jnp.dot(
-            tokens.reshape(256, 640)[:, :588], pw_ref[...], preferred_element_type=F32
+            tokens.reshape(256, 640), pw_all[...], preferred_element_type=F32
         ).reshape(8, 32, 1152)
         return (value + pb_ref[...].reshape(1, 1, 1152) + positions.astype(F32)).astype(BF16)
 
-    ready("pw", "pb")
+    ready("pb")
     resid[...] = embed(own_ref[...], pos_ref[...].reshape(1, 32, 1152)).reshape(256, 1152)
     ready("lng", "lnb", "bqkv", "wqkv")
     bias = jnp.transpose(jnp.broadcast_to(bqkv_ref[...].reshape(1, 1728), (8, 1728)))[:, 0:1]
@@ -494,7 +511,7 @@
             pltpu.SMEM((32,), jnp.int32),
             pltpu.VMEM((256, 224), BF16),
             pltpu.VMEM((224, 256), BF16),
-            pltpu.VMEM((896, 640), BF16),
+            pltpu.VMEM((640, 588), BF16),
             pltpu.VMEM((32, 1152), BF16),
             pltpu.VMEM((588, 1152), BF16),
             pltpu.VMEM((1152,), F32),
@@ -514,7 +531,7 @@
             pltpu.VMEM((2, 2, 8, 256), F32),
             pltpu.VMEM((8, 2, 8, 256), F32),
             pltpu.VMEM((8, 2, 8, 256), F32),
-            pltpu.VMEM((256, 896), BF16),
+            pltpu.VMEM((640, 1152), BF16),
             pltpu.VMEM((32, 32, 640), BF16),
             pltpu.VMEM((8, 32, 1152), BF16),
             pltpu.VMEM((8, 32, 640), BF16),
@@ -531,10 +548,12 @@
             pltpu.VMEM((8, 32, 640), BF16),
             pltpu.SemaphoreType.DMA((8,)),
             pltpu.SemaphoreType.DMA((16,)),
-            pltpu.SemaphoreType.DMA((5,)),
-            pltpu.SemaphoreType.DMA((5,)),
             pltpu.SemaphoreType.DMA((3,)),
             pltpu.SemaphoreType.DMA((3,)),
+            pltpu.SemaphoreType.DMA((2, 8)),
+            pltpu.SemaphoreType.DMA((2, 8)),
+            pltpu.SemaphoreType.DMA((3, 8)),
+            pltpu.SemaphoreType.DMA((3, 8)),
             pltpu.SemaphoreType.DMA((7,)),
             pltpu.SemaphoreType.DMA((7,)),
             pltpu.SemaphoreType.DMA((42,)),
@@ -552,7 +571,7 @@
         frame_order,
         combine_matrix(),
         column_matrix(),
-        place_matrix(),
+        order_matrix(),
         pos_embed,
         patch_weight,
         patch_bias,

time: 89.7 us -> 93 us (1.037)
  Pallas kernels: 87 us -> 91 us
    pallas_call x1, Pallas kernels: 87 us -> 91 us  [shards(): pl.pallas_call(kernel, out_shape=jax.ShapeDtypeStruct((8, 32, 1152), BF16...]
where the time goes in v4:
time: 93 us; the launch traced here: 92.9 us
  Pallas kernels  91 us (98%)
  local copies, waits for them, and re-layouts  1.92 us (2%)
    pallas_call x1, Pallas kernels, shards(): pl.pallas_call(kernel, out_shape=jax.ShapeDtypeStruct((8, 32, 1152), BF16...  91 us
    unnamed x1, local copies, waits for them, and re-layouts  1.92 us

profile of v4, /device:TPU:1, one launch (start us, length us, event | category | flops | bytes accessed | tf_op | source)
XLA Modules:
  0.0 92.9 jit_solution(11063804110776792073)
XLA Ops:
  0.0 91.0 %decoder_block.1 = bf16[8,32,1152]{2,1,0:T(8,128)(2,1)} custom-call(bf16[8,7,192,224]{3,2,1,0:T(8,128)(2,1)} %bitcast.3, bf16[3,27,192]{2,1,0:T(8,128)(2,1)} %bitcast.5, f32[192]{0:T(256)} %gain_hbm.1, f32[3]{0:T(128)} %bias_hbm.1, s32[32]{0:T(128)} %order_hbm.1, bf16[256,224]{1,0:T(8,128)(2,1)} %constant.6.clone.combine_hbm, ...), custom_call_target="tpu_custom_call" | custom-call | tf_op jit(solution)/shard_map/decoder_block/pallas_call | solution.py:501
  91.0 1.9 %copy.19 = bf16[8,32,1152]{2,1,0:T(8,128)(2,1)} copy(bf16[8,32,1152]{2,1,0:T(8,128)(2,1)} %decoder_block.1) | data formatting | bytes 1179648

commit v5 on v4

--- a/solution.py
+++ b/solution.py
@@ -17,12 +17,15 @@
 P_ORDER = [0, 13] + list(range(1, 13))
 
 
+def shifted(g, j):
+    return 1 if (g == 0 and j == 0) or (g == 1 and j == 2) else 0
+
+
 def combine_matrix():
-    m = np.zeros((256, 224), np.float32)
+    m = np.zeros((192, 224), np.float32)
     for g in range(2):
         for j in range(3):
-            shifted = 1 if (g == 0 and j == 0) or (g == 1 and j == 2) else 0
-            base = shifted * 128 + g * 64
+            base = shifted(g, j) * 96 + g * 48
             for c in range(3):
                 for at, p in enumerate(P_ORDER):
                     r, h = divmod(p, 2)
@@ -30,8 +33,17 @@
                         source = r + (h + i - 1) // 2
                         if 0 <= source < 7:
                             m[base + at * 3 + c, source * 32 + 9 * i + 3 * j + c] = 1
-                m[base + 48 + c, 6 * 32 + 3 * j + c] = 1
-                m[base + 56 + 3 + c, 18 + 3 * j + c] = 1
+    return m.astype(jnp.bfloat16)
+
+
+def edge_matrix():
+    m = np.zeros((64, 64), np.float32)
+    for g in range(2):
+        for j in range(3):
+            base = shifted(g, j) * 32 + g * 16
+            for c in range(3):
+                m[base + c, 32 + 3 * j + c] = 1
+                m[base + 8 + 3 + c, 18 + 3 * j + c] = 1
     return m.astype(jnp.bfloat16)
 
 
@@ -65,6 +77,7 @@
     bias_hbm,
     order_hbm,
     combine_hbm,
+    edge_hbm,
     column_hbm,
     perm_hbm,
     pos_hbm,
@@ -83,6 +96,7 @@
     bias_ref,
     order_ref,
     combine_ref,
+    edge_ref,
     column_ref,
     perm_ref,
     pos_ref,
@@ -123,8 +137,6 @@
     load_sem,
     near_send,
     near_recv,
-    edge_send,
-    edge_recv,
     ring_send,
     ring_recv,
     pos_send,
@@ -147,6 +159,7 @@
         "bias",
         "order",
         "combine",
+        "edge",
         "column",
         "perm",
         "pos",
@@ -165,6 +178,7 @@
         (bias_hbm, bias_ref),
         (order_hbm, order_ref),
         (combine_hbm, combine_ref),
+        (edge_hbm, edge_ref),
         (column_hbm, column_ref),
         (perm_hbm, perm_ref),
         (pos_hbm, pos_ref),
@@ -188,10 +202,24 @@
 
     loads["taps"].start()
     loads["gain"].start()
+    rows_in = [
+        pltpu.make_async_copy(x_hbm.at[:, r], x_ref.at[:, r], x_sem.at[at])
+        for at, r in ((8, 0), (9, 6))
+    ]
+
+    def inner(f):
+        return pltpu.make_async_copy(
+            x_hbm.at[f, pl.ds(1, 5)], x_ref.at[f, pl.ds(1, 5)], x_sem.at[f]
+        )
+
+    for copy in rows_in:
+        copy.start()
+    loads["edge"].start()
     for f in [6, 7, 0, 1, 2, 3, 4, 5]:
-        pltpu.make_async_copy(x_hbm.at[f], x_ref.at[f], x_sem.at[f]).start()
+        inner(f).start()
     for name in names[2:]:
-        loads[name].start()
+        if name != "edge":
+            loads[name].start()
 
     planes = [lax.rem(z + d, 8) for d in range(1, 8)]
     heads = [lax.rem(q + d, 8) for d in range(1, 8)]
@@ -220,8 +248,8 @@
     gain = jnp.transpose(jnp.broadcast_to(0.5 * gain_ref[...].reshape(1, 192), (8, 192)))[:, 0:1]
     weight = w_ref[...].reshape(96, 192).astype(BF16)
 
-    def convolve(f):
-        for r in range(7):
+    def convolve(f, which):
+        for r in which:
             x = x_ref[f, r].astype(F32)
             factor = lax.rsqrt(jnp.sum(x * x, axis=0, keepdims=True) * (1.0 / 192.0) + 1e-06)
             u = x * factor * gain
@@ -241,28 +269,37 @@
             m, low, preferred_element_type=F32
         )
         for g in range(2):
-            moved = pltpu.roll(y[128 + 64 * g : 192 + 64 * g], 1 if g == 0 else 255, 1)
-            v = y[64 * g : 64 * g + 64] + moved
-            vs[f, g] = v[0:48]
-            edn[f, g] = v[48:56]
-            eup[f, g] = v[56:64]
-
-    def late(i, carry):
-        f = i + 6
-        pltpu.make_async_copy(x_hbm.at[f], x_ref.at[f], x_sem.at[f]).wait()
-        convolve(f)
+            moved = pltpu.roll(y[96 + 48 * g : 144 + 48 * g], 1 if g == 0 else 255, 1)
+            vs[f, g] = y[48 * g : 48 * g + 48] + moved
+
+    def edge_rows(f, carry):
+        total = jnp.concatenate([acc[f, 0:32], acc[f, 192:224]], axis=0)
+        high = total.astype(BF16)
+        low = (total - high.astype(F32)).astype(BF16)
+        m = edge_ref[...]
+        y = jnp.dot(m, high, preferred_element_type=F32) + jnp.dot(
+            m, low, preferred_element_type=F32
+        )
+        for g in range(2):
+            moved = pltpu.roll(y[32 + 16 * g : 48 + 16 * g], 1 if g == 0 else 255, 1)
+            v = y[16 * g : 16 * g + 16] + moved
+            edn[f, g] = v[0:8]
+            eup[f, g] = v[8:16]
+        return carry
+
+    def outer_rows(f, carry):
+        convolve(f, (0, 6))
+        return carry
+
+    def inner_rows(f, carry):
+        inner(f).wait()
+        convolve(f, (1, 2, 3, 4, 5))
         return carry
 
     colour = lax.rem(lax.broadcasted_iota(jnp.int32, (48, 256), 0), 3)
     from_above = s > 0
     from_below = s < 63
     from_prior = t > 0
-
-    def edges(f):
-        return [
-            remote(edn.at[f], edn_in.at[f], edge_send.at[0, f], edge_recv.at[0, f], near[0]),
-            remote(eup.at[f], eup_in.at[f], edge_send.at[1, f], edge_recv.at[1, f], near[1]),
-        ]
 
     def spread(f):
         slot = t * 8 + f
@@ -278,8 +315,6 @@
         ]
 
     def finish(f):
-        for copy in edges(f):
-            copy.wait()
         bias = jnp.where(colour == 0, bias_ref[0], jnp.where(colour == 1, bias_ref[1], bias_ref[2]))
         parts = []
         for g in range(2):
@@ -287,71 +322,101 @@
                 from_below, eup_in[f, g], 0.0
             )
             v = vs[f, g] + bias
-            parts += [v[0:8] + edge, v[8:48], jnp.zeros((16, 256), F32)]
+            parts += [v[0:8] + edge, v[8:48]]
         v = jnp.concatenate(parts, axis=0).astype(BF16)
         cols = lax.dot_general(
             column_ref[...], v, (((1,), (1,)), ((), ())), preferred_element_type=F32
         )
         pieces = [
-            cols[x * 32 : (x + 1) * 32, g * 64 : g * 64 + 42] for x in range(7) for g in range(2)
+            cols[x * 32 : (x + 1) * 32, g * 48 : g * 48 + 42] for x in range(7) for g in range(2)
         ]
         pieces.append(jnp.zeros((32, 52), F32))
         gathered[t * 8 + f] = jnp.concatenate(pieces, axis=1).astype(BF16)
         for copy in spread(f):
             copy.start()
 
-    lax.fori_loop(0, 2, late, 0)
+    right = {"ha": lax.rem(z + 1, 8) * 8 + q, "ta": t}
+    left = {"ha": lax.rem(z + 7, 8) * 8 + q, "ta": t}
+
+    def relay(k, way):
+        slot = lax.rem(z + 8 - k, 8) if way == 0 else lax.rem(z + k, 8)
+        return remote(
+            pos_in.at[slot],
+            pos_in.at[slot],
+            pos_send.at[way, k],
+            pos_recv.at[way, k],
+            right if way == 0 else left,
+        )
+
+    def relay_start(k):
+        for way in (0, 1) if k < 3 else (0,):
+            relay(k, way).start()
+
+    def relay_wait(k):
+        for way in (0, 1) if k < 3 else (0,):
+            relay(k, way).wait()
+
+    for copy in rows_in:
+        copy.wait()
+    lax.fori_loop(0, 8, outer_rows, 0)
+    ready("edge", "pos")
+    lax.fori_loop(0, 10, edge_rows, 0)
+    pos_in[z] = pos_ref[...]
+    tail = pl.ds(8, 2)
+    body = pl.ds(0, 8)
+    halo = [
+        remote(edn.at[body], edn_in, near_send.at[0], near_recv.at[0], near[0]),
+        remote(eup.at[body], eup_in, near_send.at[1], near_recv.at[1], near[1]),
+        remote(edn.at[tail], edn_c, near_send.at[2], near_recv.at[2], near[2]),
+        remote(eup.at[tail], eup_c, near_send.at[3], near_recv.at[3], near[3]),
+        remote(vs.at[tail], vin, near_send.at[4], near_recv.at[4], {"ha": s, "ta": after}),
+    ]
     pl.semaphore_wait(barrier, len(peers))
+    for copy in halo[:4]:
+        copy.start()
+    relay_start(0)
+    lax.fori_loop(6, 8, inner_rows, 0)
     ready("combine")
     for f in (8, 9):
         combine(f)
-    tail = pl.ds(8, 2)
-    halo = [
-        remote(vs.at[tail], vin, near_send.at[0], near_recv.at[0], {"ha": s, "ta": after}),
-        remote(edn.at[tail], edn_c, near_send.at[1], near_recv.at[1], near[2]),
-        remote(eup.at[tail], eup_c, near_send.at[2], near_recv.at[2], near[3]),
-    ]
+    halo[4].start()
+    relay_wait(0)
+    relay_start(1)
+    lax.fori_loop(0, 2, inner_rows, 0)
+    ready("bias", "column")
+    relay_wait(1)
+    relay_start(2)
+    lax.fori_loop(2, 3, inner_rows, 0)
+    for f in range(3):
+        combine(f)
     for copy in halo:
-        copy.start()
-    ready("pos", "bias", "column")
-    pos_copies = []
-    for d in range(7):
-        copy = remote(pos_ref, pos_in.at[z], pos_send.at[d], pos_recv.at[d], column[d])
-        copy.start()
-        pos_copies.append(copy)
+        copy.wait()
+    for first in range(2):
+        for g in range(2):
+            extra = jnp.where(from_prior, vin[first, g], 0.0)
+            corner = jnp.where(from_prior & from_above, edn_c[first, g], 0.0) + jnp.where(
+                from_prior & from_below, eup_c[first, g], 0.0
+            )
+            vs[first, g] += extra
+            vs[first, g, 0:8] += corner
+
+    def finish_one(f, carry):
+        finish(f)
+        return carry
 
     def early(f, carry):
-        pltpu.make_async_copy(x_hbm.at[f], x_ref.at[f], x_sem.at[f]).wait()
-        convolve(f)
+        inner_rows(f, carry)
         combine(f)
-        for copy in edges(f):
-            copy.start()
-
-        @pl.when(f == 1)
-        def _():
-            for copy in halo:
-                copy.wait()
-            for first in range(2):
-                for g in range(2):
-                    extra = jnp.where(from_prior, vin[first, g], 0.0)
-                    corner = jnp.where(from_prior & from_above, edn_c[first, g], 0.0) + jnp.where(
-                        from_prior & from_below, eup_c[first, g], 0.0
-                    )
-                    vs[first, g] += extra
-                    vs[first, g, 0:8] += corner
-
-        @pl.when(f > 0)
-        def _():
-            finish(f - 1)
-
+        finish(f)
         return carry
 
-    lax.fori_loop(0, 6, early, 0)
+    lax.fori_loop(0, 3, finish_one, 0)
+    relay_wait(2)
+    relay_start(3)
+    lax.fori_loop(3, 6, early, 0)
     for f in (6, 7):
         combine(f)
-        for copy in edges(f):
-            copy.start()
-    lax.fori_loop(5, 8, lambda f, carry: (finish(f), carry)[1], 0)
+    lax.fori_loop(6, 8, finish_one, 0)
     ready("perm", "pw", "order")
     pw_all[...] = jnp.dot(perm_ref[...], pw_ref[...], preferred_element_type=F32).astype(BF16)
     for f in range(8):
@@ -388,9 +453,7 @@
     bias = jnp.transpose(jnp.broadcast_to(bqkv_ref[...].reshape(1, 1728), (8, 1728)))[:, 0:1]
     for copy in frames:
         copy.wait()
-    for copy in pos_copies:
-        copy.wait()
-    pos_in[z] = pos_ref[...]
+    relay_wait(3)
     value = embed(x_in[...], pos_in[...]).reshape(256, 1152).astype(F32)
     centre = jnp.mean(value, axis=-1, keepdims=True)
     value = value - centre
@@ -501,7 +564,7 @@
     return pl.pallas_call(
         kernel,
         out_shape=jax.ShapeDtypeStruct((8, 32, 1152), BF16),
-        in_specs=[hbm] * 17,
+        in_specs=[hbm] * 18,
         out_specs=vmem,
         scratch_shapes=[
             pltpu.VMEM((8, 7, 192, 224), BF16),
@@ -509,7 +572,8 @@
             pltpu.VMEM((192,), F32),
             pltpu.SMEM((3,), F32),
             pltpu.SMEM((32,), jnp.int32),
-            pltpu.VMEM((256, 224), BF16),
+            pltpu.VMEM((192, 224), BF16),
+            pltpu.VMEM((64, 64), BF16),
             pltpu.VMEM((224, 256), BF16),
             pltpu.VMEM((640, 588), BF16),
             pltpu.VMEM((32, 1152), BF16),
@@ -546,16 +610,14 @@
             pltpu.VMEM((8, 80, 256), BF16),
             pltpu.VMEM((8, 32, 640), BF16),
             pltpu.VMEM((8, 32, 640), BF16),
-            pltpu.SemaphoreType.DMA((8,)),
-            pltpu.SemaphoreType.DMA((16,)),
-            pltpu.SemaphoreType.DMA((3,)),
-            pltpu.SemaphoreType.DMA((3,)),
-            pltpu.SemaphoreType.DMA((2, 8)),
-            pltpu.SemaphoreType.DMA((2, 8)),
+            pltpu.SemaphoreType.DMA((10,)),
+            pltpu.SemaphoreType.DMA((17,)),
+            pltpu.SemaphoreType.DMA((5,)),
+            pltpu.SemaphoreType.DMA((5,)),
             pltpu.SemaphoreType.DMA((3, 8)),
             pltpu.SemaphoreType.DMA((3, 8)),
-            pltpu.SemaphoreType.DMA((7,)),
-            pltpu.SemaphoreType.DMA((7,)),
+            pltpu.SemaphoreType.DMA((2, 4)),
+            pltpu.SemaphoreType.DMA((2, 4)),
             pltpu.SemaphoreType.DMA((42,)),
             pltpu.SemaphoreType.DMA((42,)),
         ],
@@ -570,6 +632,7 @@
         head_bias,
         frame_order,
         combine_matrix(),
+        edge_matrix(),
         column_matrix(),
         order_matrix(),
         pos_embed,

time: 93 us -> 87 us (0.935)
  Pallas kernels: 91 us -> 84.9 us
    pallas_call x1, Pallas kernels: 91 us -> 84.9 us  [shards(): pl.pallas_call(kernel, out_shape=jax.ShapeDtypeStruct((8, 32, 1152), BF16...]
where the time goes in v5:
time: 87 us; the launch traced here: 86.9 us
  Pallas kernels  84.9 us (98%)
  local copies, waits for them, and re-layouts  1.92 us (2%)
    pallas_call x1, Pallas kernels, shards(): pl.pallas_call(kernel, out_shape=jax.ShapeDtypeStruct((8, 32, 1152), BF16...  84.9 us
    unnamed x1, local copies, waits for them, and re-layouts  1.92 us

profile of v5, /device:TPU:1, one launch (start us, length us, event | category | flops | bytes accessed | tf_op | source)
XLA Modules:
  0.0 86.9 jit_solution(8180513801653775047)
XLA Ops:
  0.0 84.9 %decoder_block.1 = bf16[8,32,1152]{2,1,0:T(8,128)(2,1)} custom-call(bf16[8,7,192,224]{3,2,1,0:T(8,128)(2,1)} %bitcast.3, bf16[3,27,192]{2,1,0:T(8,128)(2,1)} %bitcast.5, f32[192]{0:T(256)} %gain_hbm.1, f32[3]{0:T(128)} %bias_hbm.1, s32[32]{0:T(128)} %order_hbm.1, bf16[192,224]{1,0:T(8,128)(2,1)} %constant.8.clone.combine_hbm, ...), custom_call_target="tpu_custom_call" | custom-call | tf_op jit(solution)/shard_map/decoder_block/pallas_call | solution.py:564
  84.9 1.9 %copy.20 = bf16[8,32,1152]{2,1,0:T(8,128)(2,1)} copy(bf16[8,32,1152]{2,1,0:T(8,128)(2,1)} %decoder_block.1) | data formatting | bytes 1179648

commit v6 on v5

--- a/solution.py
+++ b/solution.py
@@ -119,7 +119,8 @@
     edn_in,
     eup_in,
     pw_all,
-    gathered,
+    gathered_a,
+    gathered_b,
     pos_in,
     own_ref,
     x_in,
@@ -301,14 +302,16 @@
     from_below = s < 63
     from_prior = t > 0
 
-    def spread(f):
+    gathered = (gathered_a, gathered_b)
+
+    def spread(half, f):
         slot = t * 8 + f
         return [
             remote(
-                gathered.at[slot],
-                gathered.at[slot],
-                ring_send.at[d, f],
-                ring_recv.at[d, f],
+                gathered[half].at[slot],
+                gathered[half].at[slot],
+                ring_send.at[half, d, f],
+                ring_recv.at[half, d, f],
                 ring[d],
             )
             for d in range(3)
@@ -331,8 +334,10 @@
             cols[x * 32 : (x + 1) * 32, g * 48 : g * 48 + 42] for x in range(7) for g in range(2)
         ]
         pieces.append(jnp.zeros((32, 52), F32))
-        gathered[t * 8 + f] = jnp.concatenate(pieces, axis=1).astype(BF16)
-        for copy in spread(f):
+        tokens = jnp.concatenate(pieces, axis=1).astype(BF16)
+        for half in range(2):
+            gathered[half][t * 8 + f] = tokens[16 * half : 16 * half + 16]
+        for copy in spread(0, f):
             copy.start()
 
     right = {"ha": lax.rem(z + 1, 8) * 8 + q, "ta": t}
@@ -380,12 +385,8 @@
     for f in (8, 9):
         combine(f)
     halo[4].start()
-    relay_wait(0)
-    relay_start(1)
     lax.fori_loop(0, 2, inner_rows, 0)
     ready("bias", "column")
-    relay_wait(1)
-    relay_start(2)
     lax.fori_loop(2, 3, inner_rows, 0)
     for f in range(3):
         combine(f)
@@ -410,96 +411,135 @@
         finish(f)
         return carry
 
+    relay_wait(0)
+    relay_start(1)
     lax.fori_loop(0, 3, finish_one, 0)
+    relay_wait(1)
+    relay_start(2)
+    lax.fori_loop(3, 6, early, 0)
     relay_wait(2)
     relay_start(3)
-    lax.fori_loop(3, 6, early, 0)
     for f in (6, 7):
         combine(f)
     lax.fori_loop(6, 8, finish_one, 0)
+    for f in range(8):
+        for copy in spread(1, f):
+            copy.start()
     ready("perm", "pw", "order")
     pw_all[...] = jnp.dot(perm_ref[...], pw_ref[...], preferred_element_type=F32).astype(BF16)
-    for f in range(8):
-        for copy in spread(f):
-            copy.wait()
-    for j in range(8):
-        own_ref[j] = gathered[order_ref[t * 8 + j]]
-
-    frames = []
-    for d in range(7):
-        copy = remote(
-            own_ref.at[planes[d]], x_in.at[z], send_sem.at[d], recv_sem.at[d], column[d]
-        )
-        copy.start()
-        frames.append(copy)
-    x_in[z] = own_ref[z]
-
-    row = lax.broadcasted_iota(jnp.int32, (80, 256), 0)
-    for h in range(8):
-        q_out[h, 0] = jnp.zeros((80, 256), BF16)
-        q_out[h, 1] = jnp.zeros((80, 256), BF16)
-        q_out[h, 2] = jnp.where(row == HD, 1.0, 0.0).astype(BF16)
+    row = lax.broadcasted_iota(jnp.int32, (80, 128), 0)
+    for half in range(2):
+        for h in range(8):
+            q_out[half, h, 0] = jnp.zeros((80, 128), BF16)
+            q_out[half, h, 1] = jnp.zeros((80, 128), BF16)
+            q_out[half, h, 2] = jnp.where(row == HD, 1.0, 0.0).astype(BF16)
     z_out[...] = jnp.zeros_like(z_out)
+    ready("pb", "lng", "lnb", "bqkv", "wqkv")
+    qkv_bias = jnp.transpose(jnp.broadcast_to(bqkv_ref[...].reshape(1, 1728), (8, 1728)))[:, 0:1]
+
+    def frames(half):
+        return [
+            remote(
+                own_ref.at[half, planes[d]],
+                x_in.at[half, z],
+                send_sem.at[7 * half + d],
+                recv_sem.at[7 * half + d],
+                column[d],
+            )
+            for d in range(7)
+        ]
+
+    def exchange(half):
+        for f in range(8):
+            for copy in spread(half, f):
+                copy.wait()
+        for j in range(8):
+            own_ref[half, j] = gathered[half][order_ref[t * 8 + j]]
+        for copy in frames(half):
+            copy.start()
+        x_in[half, z] = own_ref[half, z]
 
     def embed(tokens, positions):
         value = jnp.dot(
-            tokens.reshape(256, 640), pw_all[...], preferred_element_type=F32
-        ).reshape(8, 32, 1152)
+            tokens.reshape(128, 640), pw_all[...], preferred_element_type=F32
+        ).reshape(8, 16, 1152)
         return (value + pb_ref[...].reshape(1, 1, 1152) + positions.astype(F32)).astype(BF16)
 
-    ready("pb")
-    resid[...] = embed(own_ref[...], pos_ref[...].reshape(1, 32, 1152)).reshape(256, 1152)
-    ready("lng", "lnb", "bqkv", "wqkv")
-    bias = jnp.transpose(jnp.broadcast_to(bqkv_ref[...].reshape(1, 1728), (8, 1728)))[:, 0:1]
-    for copy in frames:
-        copy.wait()
+    def keep(half):
+        here = slice(16 * half, 16 * half + 16)
+        resid[:, here, :] = embed(own_ref[half], pos_ref[here, :].reshape(1, 16, 1152))
+
+    def normalise(half):
+        for copy in frames(half):
+            copy.wait()
+        here = slice(16 * half, 16 * half + 16)
+        value = embed(x_in[half], pos_in[:, here, :]).reshape(128, 1152).astype(F32)
+        centre = jnp.mean(value, axis=-1, keepdims=True)
+        value = value - centre
+        spread_out = jnp.mean(value * value, axis=-1, keepdims=True)
+        normed[half] = (
+            value * lax.rsqrt(spread_out + 1e-06) * lng_ref[...].reshape(1, 1152)
+            + lnb_ref[...].reshape(1, 1152)
+        ).astype(BF16)
+
+    def pair(half, kind, d):
+        at = 14 + half * 21 + kind * 7 + d
+        return remote(
+            q_out.at[half, heads[d], kind],
+            q_in.at[half, q, kind],
+            send_sem.at[at],
+            recv_sem.at[at],
+            cluster[d],
+        )
+
+    def project(half):
+        for kind in (1, 0, 2):
+            rows = slice(kind * 576, kind * 576 + 576)
+            made = (
+                lax.dot_general(
+                    wqkv_ref[rows, :],
+                    normed[half],
+                    (((1,), (1,)), ((), ())),
+                    preferred_element_type=F32,
+                )
+                + qkv_bias[rows]
+            )
+            for h in range(8):
+                q_out[half, h, kind, 0:HD] = made[h * HD : (h + 1) * HD].astype(BF16)
+            for d in range(7):
+                pair(half, kind, d).start()
+            q_in[half, q, kind] = q_out[half, q, kind]
+
+    exchange(0)
+    keep(0)
     relay_wait(3)
-    value = embed(x_in[...], pos_in[...]).reshape(256, 1152).astype(F32)
-    centre = jnp.mean(value, axis=-1, keepdims=True)
-    value = value - centre
-    spread = jnp.mean(value * value, axis=-1, keepdims=True)
-    normed[...] = (value * lax.rsqrt(spread + 1e-06) * lng_ref[...].reshape(1, 1152) + lnb_ref[...].reshape(1, 1152)).astype(BF16)
-
-    pairs = {}
-    for kind in (1, 2, 0):
-        rows = slice(kind * 576, kind * 576 + 576)
-        made = (
-            lax.dot_general(
-                wqkv_ref[rows, :], normed[...], (((1,), (1,)), ((), ())), preferred_element_type=F32
-            )
-            + bias[rows]
-        ).astype(F32)
-        for h in range(8):
-            q_out[h, kind, 0:HD] = made[h * HD : (h + 1) * HD].astype(BF16)
+    normalise(0)
+    exchange(1)
+    project(0)
+    keep(1)
+    normalise(1)
+    project(1)
+    for half in range(2):
         for d in range(7):
-            at = 7 + kind * 7 + d
-            copy = remote(
-                q_out.at[heads[d], kind],
-                q_in.at[q, kind],
-                send_sem.at[at],
-                recv_sem.at[at],
-                cluster[d],
-            )
-            copy.start()
-            pairs[kind, d] = copy
-        q_in[q, kind] = q_out[q, kind]
-
-    for d in range(7):
-        pairs[1, d].wait()
-    for p in range(8):
-        k_all[p * 256 : (p + 1) * 256, :] = jnp.transpose(q_in[p, 1].astype(F32)).astype(BF16)
-    for d in range(7):
-        pairs[2, d].wait()
-    for p in range(8):
-        v_all[:, p * 256 : (p + 1) * 256] = q_in[p, 2]
-    for d in range(7):
-        pairs[0, d].wait()
+            pair(half, 1, d).wait()
+        for p in range(8):
+            at = half * 1024 + p * 128
+            k_all[at : at + 128, :] = jnp.transpose(q_in[half, p, 1].astype(F32)).astype(BF16)
+        for d in range(7):
+            pair(half, 0, d).wait()
+    for half in range(2):
+        for d in range(7):
+            pair(half, 2, d).wait()
+        for p in range(8):
+            at = half * 1024 + p * 128
+            v_all[:, at : at + 128] = q_in[half, p, 2]
 
     rate = HD ** (-0.5) * 1.4426950408889634
 
     def attend(i, carry):
         p = lax.rem(q + 1 + i, 8)
-        scores = jnp.dot(k_all[...], q_in[p, 0], preferred_element_type=F32)
+        asked = jnp.concatenate([q_in[0, p, 0], q_in[1, p, 0]], axis=1)
+        scores = jnp.dot(k_all[...], asked, preferred_element_type=F32)
         highest = jnp.max(scores, axis=0, keepdims=True)
         weights = jnp.exp2((scores - highest) * rate).astype(BF16)
         mixed = jnp.dot(v_all[...], weights, preferred_element_type=F32)
@@ -510,8 +550,8 @@
             remote(
                 c_out.at[p],
                 c_in.at[q],
-                send_sem.at[28 + i],
-                recv_sem.at[28 + i],
+                send_sem.at[56 + i],
+                recv_sem.at[56 + i],
                 {"ha": z * 8 + p, "ta": t},
             ).start()
 
@@ -521,14 +561,16 @@
     c_in[q] = c_out[q]
     for d in range(7):
         remote(
-            c_out.at[heads[d]], c_in.at[q], send_sem.at[28 + d], recv_sem.at[28 + d], cluster[d]
+            c_out.at[heads[d]], c_in.at[q], send_sem.at[56 + d], recv_sem.at[56 + d], cluster[d]
         ).wait()
     sides = jnp.concatenate([c_in[h, 0:HD].astype(F32) for h in range(8)], axis=0)
-    z_out[:, :, 0:576] = jnp.transpose(sides).astype(BF16).reshape(8, 32, 576)
+    merged = jnp.transpose(sides).astype(BF16).reshape(2, 8, 16, 576)
+    for half in range(2):
+        z_out[:, 16 * half : 16 * half + 16, 0:576] = merged[half]
     backs = []
     for d in range(7):
         copy = remote(
-            z_out.at[planes[d]], z_in.at[z], send_sem.at[35 + d], recv_sem.at[35 + d], column[d]
+            z_out.at[planes[d]], z_in.at[z], send_sem.at[63 + d], recv_sem.at[63 + d], column[d]
         )
         copy.start()
         backs.append(copy)
@@ -539,7 +581,7 @@
     result = jnp.dot(
         z_in[...].reshape(256, 640)[:, :576], wout_ref[...], preferred_element_type=F32
     )
-    result = result + bout_ref[...].reshape(1, 1152) + resid[...].astype(F32)
+    result = result + bout_ref[...].reshape(1, 1152) + resid[...].reshape(256, 1152).astype(F32)
     out_ref[...] = result.astype(BF16).reshape(8, 32, 1152)
 
 
@@ -596,14 +638,15 @@
             pltpu.VMEM((8, 2, 8, 256), F32),
             pltpu.VMEM((8, 2, 8, 256), F32),
             pltpu.VMEM((640, 1152), BF16),
-            pltpu.VMEM((32, 32, 640), BF16),
+            pltpu.VMEM((32, 16, 640), BF16),
+            pltpu.VMEM((32, 16, 640), BF16),
             pltpu.VMEM((8, 32, 1152), BF16),
-            pltpu.VMEM((8, 32, 640), BF16),
-            pltpu.VMEM((8, 32, 640), BF16),
-            pltpu.VMEM((256, 1152), BF16),
-            pltpu.VMEM((256, 1152), BF16),
-            pltpu.VMEM((8, 3, 80, 256), BF16),
-            pltpu.VMEM((8, 3, 80, 256), BF16),
+            pltpu.VMEM((2, 8, 16, 640), BF16),
+            pltpu.VMEM((2, 8, 16, 640), BF16),
+            pltpu.VMEM((8, 32, 1152), BF16),
+            pltpu.VMEM((2, 128, 1152), BF16),
+            pltpu.VMEM((2, 8, 3, 80, 128), BF16),
+            pltpu.VMEM((2, 8, 3, 80, 128), BF16),
             pltpu.VMEM((2048, 80), BF16),
             pltpu.VMEM((80, 2048), BF16),
             pltpu.VMEM((8, 80, 256), BF16),
@@ -614,12 +657,12 @@
             pltpu.SemaphoreType.DMA((17,)),
             pltpu.SemaphoreType.DMA((5,)),
             pltpu.SemaphoreType.DMA((5,)),
-            pltpu.SemaphoreType.DMA((3, 8)),
-            pltpu.SemaphoreType.DMA((3, 8)),
+            pltpu.SemaphoreType.DMA((2, 3, 8)),
+            pltpu.SemaphoreType.DMA((2, 3, 8)),
             pltpu.SemaphoreType.DMA((2, 4)),
             pltpu.SemaphoreType.DMA((2, 4)),
-            pltpu.SemaphoreType.DMA((42,)),
-            pltpu.SemaphoreType.DMA((42,)),
+            pltpu.SemaphoreType.DMA((70,)),
+            pltpu.SemaphoreType.DMA((70,)),
         ],
         compiler_params=pltpu.CompilerParams(
             collective_id=0, has_side_effects=True, vmem_limit_bytes=60 * 1024 * 1024

time: 87 us -> 81.4 us (0.936)
  Pallas kernels: 84.9 us -> 79.4 us
    pallas_call x1, Pallas kernels: 84.9 us -> 79.4 us  [shards(): pl.pallas_call(kernel, out_shape=jax.ShapeDtypeStruct((8, 32, 1152), BF16...]
where the time goes in v6:
time: 81.4 us; the launch traced here: 81.3 us
  Pallas kernels  79.4 us (98%)
  local copies, waits for them, and re-layouts  1.92 us (2%)
    pallas_call x1, Pallas kernels, shards(): pl.pallas_call(kernel, out_shape=jax.ShapeDtypeStruct((8, 32, 1152), BF16...  79.4 us
    unnamed x1, local copies, waits for them, and re-layouts  1.92 us

profile of v6, /device:TPU:1, one launch (start us, length us, event | category | flops | bytes accessed | tf_op | source)
XLA Modules:
  0.0 81.3 jit_solution(2074738136591991668)
XLA Ops:
  0.0 79.4 %decoder_block.1 = bf16[8,32,1152]{2,1,0:T(8,128)(2,1)} custom-call(bf16[8,7,192,224]{3,2,1,0:T(8,128)(2,1)} %bitcast.3, bf16[3,27,192]{2,1,0:T(8,128)(2,1)} %bitcast.5, f32[192]{0:T(256)} %gain_hbm.1, f32[3]{0:T(128)} %bias_hbm.1, s32[32]{0:T(128)} %order_hbm.1, bf16[192,224]{1,0:T(8,128)(2,1)} %constant.8.clone.combine_hbm, ...), custom_call_target="tpu_custom_call" | custom-call | tf_op jit(solution)/shard_map/decoder_block/pallas_call | solution.py:606
  79.4 1.9 %copy.20 = bf16[8,32,1152]{2,1,0:T(8,128)(2,1)} copy(bf16[8,32,1152]{2,1,0:T(8,128)(2,1)} %decoder_block.1) | data formatting | bytes 1179648

commit v7 on v6

--- a/solution.py
+++ b/solution.py
@@ -121,7 +121,6 @@
     pw_all,
     gathered_a,
     gathered_b,
-    pos_in,
     own_ref,
     x_in,
     resid,
@@ -140,8 +139,6 @@
     near_recv,
     ring_send,
     ring_recv,
-    pos_send,
-    pos_recv,
     send_sem,
     recv_sem,
 ):
@@ -340,33 +337,11 @@
         for copy in spread(0, f):
             copy.start()
 
-    right = {"ha": lax.rem(z + 1, 8) * 8 + q, "ta": t}
-    left = {"ha": lax.rem(z + 7, 8) * 8 + q, "ta": t}
-
-    def relay(k, way):
-        slot = lax.rem(z + 8 - k, 8) if way == 0 else lax.rem(z + k, 8)
-        return remote(
-            pos_in.at[slot],
-            pos_in.at[slot],
-            pos_send.at[way, k],
-            pos_recv.at[way, k],
-            right if way == 0 else left,
-        )
-
-    def relay_start(k):
-        for way in (0, 1) if k < 3 else (0,):
-            relay(k, way).start()
-
-    def relay_wait(k):
-        for way in (0, 1) if k < 3 else (0,):
-            relay(k, way).wait()
-
     for copy in rows_in:
         copy.wait()
     lax.fori_loop(0, 8, outer_rows, 0)
-    ready("edge", "pos")
+    ready("edge")
     lax.fori_loop(0, 10, edge_rows, 0)
-    pos_in[z] = pos_ref[...]
     tail = pl.ds(8, 2)
     body = pl.ds(0, 8)
     halo = [
@@ -379,7 +354,6 @@
     pl.semaphore_wait(barrier, len(peers))
     for copy in halo[:4]:
         copy.start()
-    relay_start(0)
     lax.fori_loop(6, 8, inner_rows, 0)
     ready("combine")
     for f in (8, 9):
@@ -411,21 +385,15 @@
         finish(f)
         return carry
 
-    relay_wait(0)
-    relay_start(1)
     lax.fori_loop(0, 3, finish_one, 0)
-    relay_wait(1)
-    relay_start(2)
     lax.fori_loop(3, 6, early, 0)
-    relay_wait(2)
-    relay_start(3)
     for f in (6, 7):
         combine(f)
     lax.fori_loop(6, 8, finish_one, 0)
     for f in range(8):
         for copy in spread(1, f):
             copy.start()
-    ready("perm", "pw", "order")
+    ready("perm", "pw", "order", "pos")
     pw_all[...] = jnp.dot(perm_ref[...], pw_ref[...], preferred_element_type=F32).astype(BF16)
     row = lax.broadcasted_iota(jnp.int32, (80, 128), 0)
     for half in range(2):
@@ -440,7 +408,7 @@
     def frames(half):
         return [
             remote(
-                own_ref.at[half, planes[d]],
+                resid.at[half, planes[d]],
                 x_in.at[half, z],
                 send_sem.at[7 * half + d],
                 recv_sem.at[7 * half + d],
@@ -455,25 +423,20 @@
                 copy.wait()
         for j in range(8):
             own_ref[half, j] = gathered[half][order_ref[t * 8 + j]]
+        here = slice(16 * half, 16 * half + 16)
+        value = jnp.dot(
+            own_ref[half].reshape(128, 640), pw_all[...], preferred_element_type=F32
+        ).reshape(8, 16, 1152)
+        value = value + pb_ref[...].reshape(1, 1, 1152)
+        resid[half] = (value + pos_ref[here, :].reshape(1, 16, 1152).astype(F32)).astype(BF16)
         for copy in frames(half):
             copy.start()
-        x_in[half, z] = own_ref[half, z]
-
-    def embed(tokens, positions):
-        value = jnp.dot(
-            tokens.reshape(128, 640), pw_all[...], preferred_element_type=F32
-        ).reshape(8, 16, 1152)
-        return (value + pb_ref[...].reshape(1, 1, 1152) + positions.astype(F32)).astype(BF16)
-
-    def keep(half):
-        here = slice(16 * half, 16 * half + 16)
-        resid[:, here, :] = embed(own_ref[half], pos_ref[here, :].reshape(1, 16, 1152))
+        x_in[half, z] = resid[half, z]
 
     def normalise(half):
         for copy in frames(half):
             copy.wait()
-        here = slice(16 * half, 16 * half + 16)
-        value = embed(x_in[half], pos_in[:, here, :]).reshape(128, 1152).astype(F32)
+        value = x_in[half].reshape(128, 1152).astype(F32)
         centre = jnp.mean(value, axis=-1, keepdims=True)
         value = value - centre
         spread_out = jnp.mean(value * value, axis=-1, keepdims=True)
@@ -511,12 +474,9 @@
             q_in[half, q, kind] = q_out[half, q, kind]
 
     exchange(0)
-    keep(0)
-    relay_wait(3)
     normalise(0)
     exchange(1)
     project(0)
-    keep(1)
     normalise(1)
     project(1)
     for half in range(2):
@@ -581,8 +541,10 @@
     result = jnp.dot(
         z_in[...].reshape(256, 640)[:, :576], wout_ref[...], preferred_element_type=F32
     )
-    result = result + bout_ref[...].reshape(1, 1152) + resid[...].reshape(256, 1152).astype(F32)
-    out_ref[...] = result.astype(BF16).reshape(8, 32, 1152)
+    result = (result + bout_ref[...].reshape(1, 1152)).reshape(8, 32, 1152)
+    for half in range(2):
+        here = slice(16 * half, 16 * half + 16)
+        out_ref[:, here, :] = (result[:, here, :] + resid[half].astype(F32)).astype(BF16)
 
 
 def shards(
@@ -640,10 +602,9 @@
             pltpu.VMEM((640, 1152), BF16),
             pltpu.VMEM((32, 16, 640), BF16),
             pltpu.VMEM((32, 16, 640), BF16),
-            pltpu.VMEM((8, 32, 1152), BF16),
             pltpu.VMEM((2, 8, 16, 640), BF16),
-            pltpu.VMEM((2, 8, 16, 640), BF16),
-            pltpu.VMEM((8, 32, 1152), BF16),
+            pltpu.VMEM((2, 8, 16, 1152), BF16),
+            pltpu.VMEM((2, 8, 16, 1152), BF16),
             pltpu.VMEM((2, 128, 1152), BF16),
             pltpu.VMEM((2, 8, 3, 80, 128), BF16),
             pltpu.VMEM((2, 8, 3, 80, 128), BF16),
@@ -659,8 +620,6 @@
             pltpu.SemaphoreType.DMA((5,)),
             pltpu.SemaphoreType.DMA((2, 3, 8)),
             pltpu.SemaphoreType.DMA((2, 3, 8)),
-            pltpu.SemaphoreType.DMA((2, 4)),
-            pltpu.SemaphoreType.DMA((2, 4)),
             pltpu.SemaphoreType.DMA((70,)),
             pltpu.SemaphoreType.DMA((70,)),
         ],

time: 81.4 us -> 82.8 us (1.017)
  the two profiles are of different devices: /device:TPU:1 before, /device:TPU:6 now
where the time goes in v7:
time: 82.8 us; the launch traced here: 82.6 us
  Pallas kernels  80.7 us (97%)
  local copies, waits for them, and re-layouts  1.92 us (2%)
    pallas_call x1, Pallas kernels, shards(): pl.pallas_call(kernel, out_shape=jax.ShapeDtypeStruct((8, 32, 1152), BF16...  80.7 us
    unnamed x1, local copies, waits for them, and re-layouts  1.92 us

profile of v7, /device:TPU:6, one launch (start us, length us, event | category | flops | bytes accessed | tf_op | source)
XLA Modules:
  0.0 82.6 jit_solution(7434367204109295681)
XLA Ops:
  0.0 80.7 %decoder_block.1 = bf16[8,32,1152]{2,1,0:T(8,128)(2,1)} custom-call(bf16[8,7,192,224]{3,2,1,0:T(8,128)(2,1)} %bitcast.3, bf16[3,27,192]{2,1,0:T(8,128)(2,1)} %bitcast.5, f32[192]{0:T(256)} %gain_hbm.1, f32[3]{0:T(128)} %bias_hbm.1, s32[32]{0:T(128)} %order_hbm.1, bf16[192,224]{1,0:T(8,128)(2,1)} %constant.8.clone.combine_hbm, ...), custom_call_target="tpu_custom_call" | custom-call | tf_op jit(solution)/shard_map/decoder_block/pallas_call | solution.py:568
  80.7 1.9 %copy.20 = bf16[8,32,1152]{2,1,0:T(8,128)(2,1)} copy(bf16[8,32,1152]{2,1,0:T(8,128)(2,1)} %decoder_block.1) | data formatting | bytes 1179648

commit v8 on v6

--- a/solution.py
+++ b/solution.py
@@ -411,17 +411,17 @@
         finish(f)
         return carry
 
+    lax.fori_loop(0, 3, finish_one, 0)
     relay_wait(0)
     relay_start(1)
-    lax.fori_loop(0, 3, finish_one, 0)
+    lax.fori_loop(3, 6, early, 0)
     relay_wait(1)
     relay_start(2)
-    lax.fori_loop(3, 6, early, 0)
-    relay_wait(2)
-    relay_start(3)
     for f in (6, 7):
         combine(f)
     lax.fori_loop(6, 8, finish_one, 0)
+    relay_wait(2)
+    relay_start(3)
     for f in range(8):
         for copy in spread(1, f):
             copy.start()

time: 81.4 us -> 80.8 us (level)
  no operation moved by 1% of the time
where the time goes in v8:
time: 80.8 us; the launch traced here: 80.7 us
  Pallas kernels  78.8 us (98%)
  local copies, waits for them, and re-layouts  1.92 us (2%)
    pallas_call x1, Pallas kernels, shards(): pl.pallas_call(kernel, out_shape=jax.ShapeDtypeStruct((8, 32, 1152), BF16...  78.8 us
    unnamed x1, local copies, waits for them, and re-layouts  1.92 us

profile of v8, /device:TPU:1, one launch (start us, length us, event | category | flops | bytes accessed | tf_op | source)
XLA Modules:
  0.0 80.7 jit_solution(5037838781773962850)
XLA Ops:
  0.0 78.8 %decoder_block.1 = bf16[8,32,1152]{2,1,0:T(8,128)(2,1)} custom-call(bf16[8,7,192,224]{3,2,1,0:T(8,128)(2,1)} %bitcast.3, bf16[3,27,192]{2,1,0:T(8,128)(2,1)} %bitcast.5, f32[192]{0:T(256)} %gain_hbm.1, f32[3]{0:T(128)} %bias_hbm.1, s32[32]{0:T(128)} %order_hbm.1, bf16[192,224]{1,0:T(8,128)(2,1)} %constant.8.clone.combine_hbm, ...), custom_call_target="tpu_custom_call" | custom-call | tf_op jit(solution)/shard_map/decoder_block/pallas_call | solution.py:606
  78.8 1.9 %copy.20 = bf16[8,32,1152]{2,1,0:T(8,128)(2,1)} copy(bf16[8,32,1152]{2,1,0:T(8,128)(2,1)} %decoder_block.1) | data formatting | bytes 1179648
